TPU v7x, 32 devices: a whole 2x2x4 slice. The times are simulated.
32 devices in a mesh: row: 8 (over z, x), chan: 4 (over y, core).
Axes of the slice: x: 2, y: 2, z: 4, core: 2. Of those that a mesh axis runs over, the one named last changes fastest.
Arguments:
- image: bfloat16 [32, 4096, 4096], P('chan', 'row'), may hold values from -6 to 6
- spec_weight: bfloat16 [2, 256, 32, 32, 256], P(None, 'row', None, 'chan'), may hold values from -0.75 to 0.75
- point_weight: bfloat16 [32, 32], replicated, may hold values from -1 to 1
- bias: float32 [32], P('chan'), may hold values from -3 to 3
Outputs:
- layer_out: bfloat16 [32, 4096, 4096], P('chan', 'row')
All inputs are finite; a program needn't handle non-finite values.
Results may differ from a plain program's by a relative error of at most 0.012.
Values may be sent and summed in bfloat16 or wider, within the bound.
A program may use at most 384 MiB of HBM per device.

v0:
```python
import math

import jax
import jax.numpy as jnp
from jax import lax
from jax.sharding import PartitionSpec as P

H = 4096
W = 4096
MX = 256
MY = 256


def wave_table(points, freqs, length):
    prod = jnp.mod(points[:, None] * freqs[None, :], length)
    angle = prod.astype(jnp.float32) * (2.0 * math.pi / length)
    return (jnp.cos(angle), jnp.sin(angle))


def on_device(image, spec_weight, point_weight, bias):
    chan_count, row_count, width_len = image.shape
    row_index = lax.axis_index("row")
    row_devs = lax.axis_size("row")
    chan_index = lax.axis_index("chan")
    row_global = row_index * row_count + jnp.arange(row_count, dtype=jnp.int32)
    col_pts = jnp.arange(W, dtype=jnp.int32)
    col_freq = jnp.arange(MY, dtype=jnp.int32)
    cos_w, sin_w = wave_table(col_pts, col_freq, W)
    fwd_cols = jnp.concatenate([cos_w, -sin_w], 1).astype(jnp.bfloat16)
    back_cols = jnp.concatenate([cos_w.T, -sin_w.T], 0).astype(jnp.bfloat16)
    row_freq = jnp.arange(MX, dtype=jnp.int32) - MX // 2
    colspec = jnp.dot(
        image.reshape(chan_count * row_count, width_len),
        fwd_cols,
        preferred_element_type=jnp.float32,
    )
    colspec = (
        (colspec * (1.0 / math.sqrt(W))).astype(jnp.bfloat16).reshape(chan_count, row_count, 2 * MY)
    )
    block_len = MX // row_devs
    cos_h, sin_h = wave_table(row_global, row_freq, H)
    fwd_rows = jnp.concatenate([cos_h, sin_h], 1).astype(jnp.bfloat16)
    partial_value = jnp.einsum("chp,hq->cqp", colspec, fwd_rows, preferred_element_type=jnp.float32)
    spec_re = partial_value[:, :MX, :MY] + partial_value[:, MX:, MY:]
    spec_im = partial_value[:, :MX, MY:] - partial_value[:, MX:, :MY]
    partial_value = jnp.concatenate([spec_re, spec_im], -1) * (1.0 / math.sqrt(H))
    summed = lax.psum(partial_value, "row")
    block = lax.dynamic_slice_in_dim(summed, row_index * block_len, block_len, 1)
    spectrum = block.astype(jnp.bfloat16)
    all_inputs = lax.all_gather(spectrum, "chan", axis=0, tiled=True)
    zed_re = all_inputs[..., :MY].astype(jnp.float32)
    zed_im = all_inputs[..., MY:].astype(jnp.float32)
    wgt_re = spec_weight[0].astype(jnp.float32)
    wgt_im = spec_weight[1].astype(jnp.float32)
    mix_re = jnp.einsum("kiop,ikp->okp", wgt_re, zed_re) - jnp.einsum(
        "kiop,ikp->okp", wgt_im, zed_im
    )
    mix_im = jnp.einsum("kiop,ikp->okp", wgt_re, zed_im) + jnp.einsum(
        "kiop,ikp->okp", wgt_im, zed_re
    )
    mixed = jnp.concatenate([mix_re, mix_im], -1).astype(jnp.bfloat16)
    piece = lax.all_gather(mixed, "row", axis=1, tiled=True)
    freq_now = jnp.arange(piece.shape[1], dtype=jnp.int32) - MX // 2
    cos_back, sin_back = wave_table(freq_now, row_global, H)
    with_cos = jnp.einsum(
        "okp,kh->ohp", piece, cos_back.astype(jnp.bfloat16), preferred_element_type=jnp.float32
    )
    with_sin = jnp.einsum(
        "okp,kh->ohp", piece, sin_back.astype(jnp.bfloat16), preferred_element_type=jnp.float32
    )
    back_re = with_cos[..., :MY] - with_sin[..., MY:]
    back_im = with_sin[..., :MY] + with_cos[..., MY:]
    back_re, back_im = (back_re, back_im)
    rowback = (jnp.concatenate([back_re, back_im], -1) * (1.0 / math.sqrt(MX))).astype(jnp.bfloat16)
    spectral = jnp.dot(
        rowback.reshape(chan_count * row_count, 2 * MY),
        back_cols,
        preferred_element_type=jnp.float32,
    )
    spectral = (spectral * (1.0 / math.sqrt(MY))).reshape(chan_count, row_count, width_len)
    piece = lax.all_gather(image, "chan", axis=0, tiled=True)
    weight_cols = lax.dynamic_slice(
        point_weight, (chan_index * chan_count, 0), (chan_count, piece.shape[0])
    )
    pointwise = jnp.einsum(
        "oi,ihw->ohw", weight_cols, piece, preferred_element_type=jnp.float32
    ).astype(jnp.bfloat16)
    total = spectral + pointwise.astype(jnp.float32) + bias[:, None, None]
    return jax.nn.gelu(total, approximate=False).astype(jnp.bfloat16)


def solution(mesh):
    in_specs = (P("chan", "row", None), P(None, "row", None, "chan", None), P(), P("chan"))
    out_specs = P("chan", "row", None)
    return jax.shard_map(
        on_device, mesh=mesh, in_specs=in_specs, out_specs=out_specs, check_vma=False
    )
```

profile of v0, /device:TPU:0, one launch (start us, length us, event | category | flops | bytes accessed | tf_op | source)
XLA Modules:
  0.0 1280.7 jit_solution(8275477360198457283)
XLA Ops:
  6.5 0.0 copy-start
  6.5 0.0 all-gather.4.cloned.1.call-start
  6.5 17.8 %negate_convert_fusion.1 = (bf16[4096,256]{1,0:T(8,128)(2,1)S(1)}, bf16[4096,256]{1,0:T(8,128)(2,1)}) fusion(), kind=kLoop, calls=%fused_computation.62 | loop fusion | flops 17825792 | bytes 4194304 | tf_op jit(solution)/shard_map/convert.7
  24.4 2.5 cosine_convert_fusion.2
  26.9 22.5 %multiply_convert_fusion = bf16[512,4096]{1,0:T(8,128)(2,1)S(1)} fusion(bf16[4096,4096]{1,0:T(8,128)(2,1)} %bitcast.64, bf16[4096,256]{1,0:T(8,128)(2,1)S(1)} %get-tuple-element.19, bf16[4096,256]{1,0:T(8,128)(2,1)} %get-tuple-element.20), kind=kOutput, calls=%fused_computation.32 | convolution fusion | flops 17192452096 | bytes 41943040 | tf_op jit(solution)/shard_map/dot_general | solution.py:32
  49.4 2.4 fusion.39
  51.8 0.6 slice_add_fusion.1
  52.4 2.6 maximum_multiply_fusion.1
  55.0 168.6 %all-reduce.1 = bf16[8,256,512]{2,1,0:T(8,128)(2,1)S(1)} all-reduce(f32[8,256,512]{2,1,0:T(8,128)} %maximum_multiply_fusion.1), channel_id=1, replica_groups=mesh['row'=8,'chan'=4] {'row'}, use_global_device_ids=true, to_apply=%region_0.1 | all-reduce | flops 1048576 | bytes 6291456 | tf_op jit(solution)/shard_map/psum | solution.py:47
  223.6 0.7 dynamic-slice_convert_fusion
  224.3 0.0 all-gather.4.cloned.1.call-update
  224.4 0.2 all-gather.6.cloned.1.call-start
  224.6 15.4 %all-gather.4.cloned.1.call-done = bf16[32,32,512]{2,1,0:T(8,128)(2,1)} async-done(((bf16[8,32,512]{2,1,0:T(8,128)(2,1)}), bf16[32,32,512]{2,1,0:T(8,128)(2,1)}) %all-gather.4.cloned.1.call-update) | async-done | bytes 1048592 | tf_op jit(solution)/shard_map/all_gather | solution.py:50
  240.0 1.4 fusion.48
  241.4 0.6 copy.53
  242.0 0.6 copy.52
  242.6 5.9 fusion.11
  248.6 0.1 fusion.60
  248.8 0.1 fusion.61
  248.9 0.7 pad_maximum_fusion
  249.6 0.0 all-gather.6.cloned.1.call-update
  249.7 0.0 all-gather.8.cloned.1.call-start
  249.7 29.4 %copy.16 = bf16[8,512,4096]{2,0,1:T(8,128)(2,1)} copy(bf16[8,512,4096]{2,1,0:T(8,128)(2,1)} %param.4) | data formatting | bytes 67108864 | tf_op args[0]
  279.1 0.0 all-gather.8.cloned.1.call-update
  279.1 17.6 %negate_convert_fusion = (bf16[256,4096]{1,0:T(8,128)(2,1)S(1)}, bf16[256,4096]{1,0:T(8,128)(2,1)}) fusion(), kind=kLoop, calls=%fused_computation.57 | loop fusion | flops 17825792 | bytes 4194304 | tf_op jit(solution)/shard_map/convert.1
  296.8 2.4 all-gather.6.cloned.1.call-done
  299.1 0.0 copy-start.2
  299.1 7.4 convolution_bitcast_fusion
  306.5 0.0 copy-done.2
  306.5 7.7 convolution_bitcast_fusion.1
  314.2 19.4 %slice_subtract_fusion = (f32[8,512,256]{2,1,0:T(8,128)}, f32[8,512,256]{2,1,0:T(8,128)}) fusion(f32[8,512,512]{2,1,0:T(8,128)} %convolution_bitcast_fusion, f32[8,512,512]{2,1,0:T(8,128)} %convolution_bitcast_fusion.1), kind=kLoop, calls=%fused_computation.49 | loop fusion | flops 2097152 | bytes 25165824 | tf_op jit(solution)/shard_map/sub | solution.py:71
  333.7 0.0 copy-start.3
  333.7 53.1 %convolution_multiply_fusion = f32[4096,4096]{1,0:T(8,128)} fusion(f32[4096,256]{1,0:T(8,128)} %bitcast.67, f32[4096,256]{1,0:T(8,128)} %bitcast.66, bf16[256,4096]{1,0:T(8,128)(2,1)S(1)} %get-tuple-element.21, bf16[256,4096]{1,0:T(8,128)(2,1)} %get-tuple-element.22), kind=kOutput, calls=%fused_computation.21 | convolution fusion | flops 17211326464 | bytes 79691776 | tf_op jit(solution)/shard_map/dot_general | solution.py:75
  386.8 687.6 %all-gather.8.cloned.1.call-done = bf16[32,512,4096]{2,0,1:T(8,128)(2,1)} async-done(((bf16[8,512,4096]{2,0,1:T(8,128)(2,1)}), bf16[32,512,4096]{2,0,1:T(8,128)(2,1)}) %all-gather.8.cloned.1.call-update) | async-done | bytes 134217744 | tf_op jit(solution)/shard_map/all_gather | solution.py:81
  1074.3 0.0 copy-done
  1074.4 0.0 copy-done.3
  1074.4 170.5 %fusion.2 = bf16[8,512,4096]{2,0,1:T(8,128)(2,1)} fusion(f32[8,512,4096]{2,1,0:T(8,128)} %bitcast.26, f32[8]{0:T(128)S(1)} %copy-done.3, bf16[32,512,4096]{2,0,1:T(8,128)(2,1)} %all-gather.8.cloned.1.call-done, bf16[32,32]{1,0:T(8,128)(2,1)S(1)} %copy-done, s32[]{:T(128)S(6)} %select_n.38), kind=kOutput, calls=%fused_computation.3 | convolution fusion | flops 2231369728 | bytes 234883584 | tf_op jit(solution)/shard_map/oi,ihw->ohw/dot_general | solution.py:85
  1244.8 0.0 copy-start.1
  1244.8 29.3 %copy.18 = bf16[8,512,4096]{2,1,0:T(8,128)(2,1)} copy(bf16[8,512,4096]{2,0,1:T(8,128)(2,1)} %fusion.2) | data formatting | bytes 67108864 | tf_op jit(solution)/shard_map/convert_element_type | solution.py:89
  1274.2 0.0 copy-done.1
  (2 shorter events, 0.0 us)
Async XLA Ops:
  6.5 1067.8 %copy-start = (bf16[32,32]{1,0:T(8,128)(2,1)S(1)}, bf16[32,32]{1,0:T(8,128)(2,1)}, u32[]{:S(2)}) copy-start(bf16[32,32]{1,0:T(8,128)(2,1)} %param.6) | copy-start | bytes 6148
  6.5 233.4 %all-gather.4.cloned.1.call-start = ((), (), s32[]{:S(2)}) async-start(), calls=%async_computation | async-start | bytes 1310720 | tf_op jit(solution)/shard_map/all_gather | solution.py:50
  224.4 74.8 %all-gather.6.cloned.1.call-start = ((), (), s32[]{:S(2)}) async-start(), calls=%async_computation.1 | async-start | bytes 2359296 | tf_op jit(solution)/shard_map/all_gather | solution.py:62
  249.7 824.7 %all-gather.8.cloned.1.call-start = ((), (), s32[]{:S(2)}) async-start(), calls=%async_computation.2 | async-start | bytes 167772160 | tf_op jit(solution)/shard_map/all_gather | solution.py:81
  299.1 7.4 copy-start.2
  333.7 740.7 %copy-start.3 = (f32[8]{0:T(128)S(1)}, f32[8]{0:T(128)}, u32[]{:S(2)}) copy-start(f32[8]{0:T(128)} %param.7) | copy-start | bytes 100
  1244.8 29.3 %copy-start.1 = (bf16[32,32]{1,0:T(8,128)(2,1)S(1)}, bf16[32,32]{1,0:T(8,128)(2,1)}, u32[]{:S(2)}) copy-start(bf16[32,32]{1,0:T(8,128)(2,1)} %param.6) | copy-start | bytes 6148
Sparse Core Ops, SparseCore 0:
  224.5 15.4 all-gather.3
  249.8 49.2 all-gather.5
  300.7 773.5 all-gather.7
where the time goes:
time: 1280 us
  waiting for transfers between devices  705 us (55%)
  matrix products  264 us (21%)
  blocking collectives  169 us (13%)
  other arithmetic  69 us (5%)
  local copies, waits for them, and re-layouts  60.7 us (5%)
  between operations  13.2 us (1%)
    all_gather x1, waiting for transfers between devices, on_device(): piece = lax.all_gather(image, 'chan', axis=0, tiled=True)  688 us
    dot_general x1, matrix products, on_device(): jnp.einsum('oi,ihw->ohw', weight_cols, piece, preferred_element_type=jnp....  170 us
    psum x1, blocking collectives, on_device(): summed = lax.psum(partial_value, 'row')  169 us
    dot_general x1, matrix products, on_device(): jnp.dot(rowback.reshape(chan_count * row_count, 2 * MY), back_cols, prefe...  53.1 us
    another operation x3, other arithmetic  38 us
    unnamed x11, local copies, waits for them, and re-layouts  30.6 us
    convert_element_type x1, local copies, waits for them, and re-layouts, on_device(): return jax.nn.gelu(total, approximate=False).astype(jnp.bfloat16)  29.3 us
  transfers between devices with their start and end apart: 3, of which 3 were waited for; matrix products, arithmetic and copies ran while one was open for 11% of the time, Pallas kernels for 0%

commit v1 on v0

v1 whole, which is shorter than its diff:
```python
import math

import jax
import jax.numpy as jnp
from jax import lax
from jax.experimental import pallas as pl
from jax.experimental.pallas import tpu as pltpu
from jax.sharding import PartitionSpec as P

MX = 256
MY = 256
UNIT = 16
SLACK = 5


def wave_table(points, freqs, length):
    prod = jnp.mod(points[:, None] * freqs[None, :], length)
    angle = prod.astype(jnp.float32) * (2.0 * math.pi / length)
    return (jnp.cos(angle), jnp.sin(angle))


def chunk_rows(row_count):
    if row_count >= 512:
        middle, rest = divmod(row_count - 128, 64)
        sizes = [32] + [64] * middle + [48, 32, 16] + [UNIT] * (rest // UNIT)
    else:
        sizes = [UNIT] * (row_count // UNIT)
    starts = [sum(sizes[:n]) for n in range(len(sizes))]
    return list(zip(starts, sizes))


def partial_kernel(one_ref, two_ref, kron_ref, *out_refs):
    chans, rows, width = one_ref.shape
    half = chans * rows
    tile = 1024

    @pl.loop(0, width // tile)
    def _(step):
        cols = pl.ds(pl.multiple_of(step * tile, tile), tile)
        both = jnp.concatenate(
            [one_ref[:, :, cols].reshape(half, tile), two_ref[:, :, cols].reshape(half, tile)], 0
        )
        part = jnp.dot(kron_ref[...], both, preferred_element_type=jnp.float32)
        part = part.astype(jnp.bfloat16)
        for n, out_ref in enumerate(out_refs):
            out_ref[:, :, cols] = part[n * half : (n + 1) * half].reshape(chans, rows, tile)


def partials(one, two, kron, start, rows):
    chans, _, width = one.shape
    first = start // UNIT
    block = (chans, UNIT, width)
    count = kron.shape[0] // (chans * UNIT)
    shape = jax.ShapeDtypeStruct((chans, rows, width), jnp.bfloat16)
    return pl.pallas_call(
        partial_kernel,
        grid=(rows // UNIT,),
        in_specs=[
            pl.BlockSpec(block, lambda t: (0, first + t, 0)),
            pl.BlockSpec(block, lambda t: (0, t, 0)),
            pl.BlockSpec(kron.shape, lambda t: (0, 0)),
        ],
        out_specs=[pl.BlockSpec(block, lambda t: (0, t, 0))] * count,
        out_shape=[shape] * count,
        compiler_params=pltpu.CompilerParams(vmem_limit_bytes=32 << 20),
        cost_estimate=pl.CostEstimate(
            flops=2 * count * chans * rows * width * kron.shape[1],
            bytes_accessed=(2 + count) * chans * rows * width * 2,
            transcendentals=0,
        ),
    )(one, two, kron)


def final_kernel(bias_ref, back_ref, cols_ref, home_ref, came_ref, *rest):
    out_ref = rest[-1]
    chans, rows, width = home_ref.shape
    tile = 512
    flat = back_ref[...].reshape(chans * rows, back_ref.shape[2])
    bias = bias_ref[...].reshape(chans, 1, 1)

    @pl.loop(0, width // tile)
    def _(step):
        cols = pl.ds(pl.multiple_of(step * tile, tile), tile)
        spectral = jnp.dot(flat, cols_ref[:, cols], preferred_element_type=jnp.float32)
        total = spectral.reshape(chans, rows, tile) + bias
        total += home_ref[:, :, cols].astype(jnp.float32)
        total += came_ref[:, :, cols].astype(jnp.float32)
        value = 0.5 * total * (1.0 + lax.erf(total * math.sqrt(0.5)))
        out_ref[:, :, cols] = value.astype(jnp.bfloat16)


def finish(bias, rowback, back_cols, home, came, start, held):
    chans, rows, width = home.shape
    row_count = rowback.shape[1]
    tall = 32 if rows % 32 == 0 and start % 32 == 0 else UNIT
    first = start // tall
    block = (chans, tall, width)
    in_specs = [
        pl.BlockSpec((chans, 1), lambda t: (0, 0)),
        pl.BlockSpec((chans, tall, 2 * MY), lambda t: (0, first + t, 0)),
        pl.BlockSpec(back_cols.shape, lambda t: (0, 0)),
        pl.BlockSpec(block, lambda t: (0, t, 0)),
        pl.BlockSpec(block, lambda t: (0, t, 0)),
    ]
    operands = [bias, rowback, back_cols, home, came]
    aliases = {}
    if held is not None:
        in_specs.append(pl.BlockSpec(memory_space=pl.ANY))
        operands.append(held)
        aliases = {5: 0}
    size = chans * rows * width
    return pl.pallas_call(
        final_kernel,
        grid=(rows // tall,),
        in_specs=in_specs,
        out_specs=pl.BlockSpec(block, lambda t: (0, first + t, 0)),
        out_shape=jax.ShapeDtypeStruct((chans, row_count, width), jnp.bfloat16),
        input_output_aliases=aliases,
        compiler_params=pltpu.CompilerParams(vmem_limit_bytes=48 << 20),
        cost_estimate=pl.CostEstimate(
            flops=2 * size * 2 * MY, bytes_accessed=3 * size * 2, transcendentals=size
        ),
    )(*operands)


def on_device(image, spec_weight, point_weight, bias):
    chan_count, row_count, width_len = image.shape
    row_index = lax.axis_index("row")
    row_devs = lax.axis_size("row")
    chan_devs = lax.axis_size("chan")
    chan_index = lax.axis_index("chan")
    full_rows = row_count * row_devs

    core_swap = [(c, c ^ 1) for c in range(chan_devs)]
    chip_swap = [(c, c ^ 2) for c in range(chan_devs)]
    chunks = chunk_rows(row_count)
    first_mine = lax.slice_in_dim(image, 0, chunks[0][1], axis=1)
    first_far = lax.ppermute(first_mine, "chan", chip_swap)
    first_mine, image = lax.optimization_barrier((first_mine, image))
    peers = [lax.ppermute(first_mine, "chan", core_swap)]
    for start, rows in chunks[1:]:
        mine = lax.slice_in_dim(image, start, start + rows, axis=1)
        peers.append(lax.ppermute(mine, "chan", core_swap))

    def kron(out_dev, in_dev):
        eye = jnp.eye(UNIT, dtype=jnp.bfloat16)
        blocks = [
            lax.dynamic_slice(
                point_weight, (out_dev * chan_count, dev * chan_count), (chan_count, chan_count)
            )
            for dev in (in_dev, in_dev ^ 1)
        ]
        small = jnp.concatenate(blocks, 1)
        large = small[:, None, :, None] * eye[None, :, None, :]
        return large.reshape(chan_count * UNIT, 2 * chan_count * UNIT)

    kron_home = kron(chan_index, chan_index)
    kron_far = kron(chan_index, chan_index ^ 2)
    kron_both = jnp.concatenate([kron(chan_index ^ 2, chan_index), kron_home], 0)

    row_global = row_index * row_count + jnp.arange(row_count, dtype=jnp.int32)
    col_pts = jnp.arange(width_len, dtype=jnp.int32)
    col_freq = jnp.arange(MY, dtype=jnp.int32)
    cos_w, sin_w = wave_table(col_pts, col_freq, width_len)
    fwd_cols = jnp.concatenate([cos_w, -sin_w], 1).astype(jnp.bfloat16)
    back_cols = jnp.concatenate([cos_w.T, -sin_w.T], 0).astype(jnp.bfloat16)
    back_cols = back_cols * jnp.bfloat16(1.0 / math.sqrt(MY))
    row_freq = jnp.arange(MX, dtype=jnp.int32) - MX // 2
    colspec = jnp.dot(
        image.reshape(chan_count * row_count, width_len),
        fwd_cols,
        preferred_element_type=jnp.float32,
    )
    colspec = (
        (colspec * (1.0 / math.sqrt(width_len)))
        .astype(jnp.bfloat16)
        .reshape(chan_count, row_count, 2 * MY)
    )
    cos_h, sin_h = wave_table(row_global, row_freq, full_rows)
    fwd_rows = jnp.concatenate([cos_h, sin_h], 1).astype(jnp.bfloat16)
    partial_value = jnp.einsum("chp,hq->cqp", colspec, fwd_rows, preferred_element_type=jnp.float32)
    spec_re = partial_value[:, :MX, :MY] + partial_value[:, MX:, MY:]
    spec_im = partial_value[:, :MX, MY:] - partial_value[:, MX:, :MY]
    partial_value = jnp.concatenate([spec_re, spec_im], -1) * (1.0 / math.sqrt(full_rows))
    block = lax.psum_scatter(partial_value, "row", scatter_dimension=1, tiled=True)
    spectrum = block.astype(jnp.bfloat16)
    all_inputs = lax.all_gather(spectrum, "chan", axis=0, tiled=True)
    zed_re = all_inputs[..., :MY].astype(jnp.float32)
    zed_im = all_inputs[..., MY:].astype(jnp.float32)
    wgt_re = spec_weight[0].astype(jnp.float32)
    wgt_im = spec_weight[1].astype(jnp.float32)
    mix_re = jnp.einsum("kiop,ikp->okp", wgt_re, zed_re) - jnp.einsum(
        "kiop,ikp->okp", wgt_im, zed_im
    )
    mix_im = jnp.einsum("kiop,ikp->okp", wgt_re, zed_im) + jnp.einsum(
        "kiop,ikp->okp", wgt_im, zed_re
    )
    mixed = jnp.concatenate([mix_re, mix_im], -1).astype(jnp.bfloat16)
    piece = lax.all_gather(mixed, "row", axis=1, tiled=True)
    cos_back = cos_h.T.astype(jnp.bfloat16)
    sin_back = sin_h.T.astype(jnp.bfloat16)
    with_cos = jnp.einsum("okp,kh->ohp", piece, cos_back, preferred_element_type=jnp.float32)
    with_sin = jnp.einsum("okp,kh->ohp", piece, sin_back, preferred_element_type=jnp.float32)
    back_re = with_cos[..., :MY] - with_sin[..., MY:]
    back_im = with_sin[..., :MY] + with_cos[..., MY:]
    rowback = (jnp.concatenate([back_re, back_im], -1) * (1.0 / math.sqrt(MX))).astype(jnp.bfloat16)

    bias = bias[:, None]
    held = None
    homes, cames = [], []
    done = 0

    def finish_next():
        return finish(bias, rowback, back_cols, homes[done], cames[done], chunks[done][0], held)

    for n, (start, rows) in enumerate(chunks):
        if n == 0:
            first_other = lax.ppermute(first_far, "chan", core_swap)
            homes += partials(image, peers[0], kron_home, start, rows)
            cames += partials(first_far, first_other, kron_far, 0, rows)
            continue
        away, home = partials(image, peers[n], kron_both, start, rows)
        if n >= 2:
            before = first_far if n == 2 else cames[n - 2]
            away, before = lax.optimization_barrier((away, before))
            if n > 2:
                cames[n - 2] = before
        if n >= SLACK:
            while done <= n - 3:
                held = finish_next()
                done += 1
            away, held = lax.optimization_barrier((away, held))
        homes.append(home)
        cames.append(lax.ppermute(away, "chan", chip_swap))
    while done < len(chunks):
        held = finish_next()
        done += 1
    return held


def solution(mesh):
    in_specs = (P("chan", "row", None), P(None, "row", None, "chan", None), P(), P("chan"))
    out_specs = P("chan", "row", None)
    return jax.shard_map(
        on_device, mesh=mesh, in_specs=in_specs, out_specs=out_specs, check_vma=False
    )
```

time: 1280 us -> 845 us (0.66)
  waiting for transfers between devices: 705 us -> 475 us
  matrix products: 264 us -> 37.9 us
  Pallas kernels: 0 us -> 172 us
  blocking collectives: 169 us -> 0 us
  starting transfers between devices: 0.27 us -> 17.9 us
    all_gather x1 -> x0, waiting for transfers between devices: 688 us -> none  [on_device(): piece = lax.all_gather(image, 'chan', axis=0, tiled=True)]
    ppermute x0 -> x21, waiting for transfers between devices: none -> 423 us  [the longest x9 341 us: on_device(): cames.append(lax.ppermute(away, 'chan', chip_swap))]
    dot_general x4 -> x2, matrix products: 239 us -> 12.7 us  [the longest x1 7.24 us: on_device(): jnp.einsum('okp,kh->ohp', piece, cos_back, preferred_element_type=jnp.flo...]
    pallas_call x0 -> x21, Pallas kernels: none -> 172 us  [the longest x10 103 us: finish(): pl.pallas_call(final_kernel, grid=(rows // tall,), in_specs=in_specs, out...]
    psum x1 -> x0, blocking collectives: 169 us -> none  [on_device(): summed = lax.psum(partial_value, 'row')]
    reduce_scatter x0 -> x1, waiting for transfers between devices: none -> 52.1 us  [on_device(): lax.psum_scatter(partial_value, 'row', scatter_dimension=1, tiled=True)]
    convert_element_type x1 -> x0, local copies, waits for them, and re-layouts: 29.3 us -> none  [on_device(): return jax.nn.gelu(total, approximate=False).astype(jnp.bfloat16)]
    slice x0 -> x5, local copies, waits for them, and re-layouts: none -> 29 us  [the longest x4 25.9 us: on_device(): mine = lax.slice_in_dim(image, start, start + rows, axis=1)]
  transfers between devices with their start and end apart: 3 -> 24, of which waited for: 3 -> 11; matrix products, arithmetic and copies ran while one was open for 11% -> 10% of each run, Pallas kernels for 0% -> 20%
where the time goes in v1:
time: 845 us; the launch traced here: 844 us
  waiting for transfers between devices  475 us (56%)
  Pallas kernels  172 us (20%)
  other arithmetic  68.8 us (8%)
  local copies, waits for them, and re-layouts  58.4 us (7%)
  matrix products  37.9 us (4%)
  starting transfers between devices  17.9 us (2%)
  between operations  13.4 us (2%)
    ppermute x9, waiting for transfers between devices, on_device(): cames.append(lax.ppermute(away, 'chan', chip_swap))  341 us
    pallas_call x10, Pallas kernels, finish(): pl.pallas_call(final_kernel, grid=(rows // tall,), in_specs=in_specs, out...  103 us
    ppermute x1, waiting for transfers between devices, on_device(): first_far = lax.ppermute(first_mine, 'chan', chip_swap)  76.7 us
    pallas_call x11, Pallas kernels, partials(): pl.pallas_call(partial_kernel, grid=(rows // UNIT,), in_specs=[pl.BlockSp...  68.9 us
    reduce_scatter x1, waiting for transfers between devices, on_device(): lax.psum_scatter(partial_value, 'row', scatter_dimension=1, tiled=True)  52.1 us
    another operation x3, other arithmetic  37.2 us
    slice x4, local copies, waits for them, and re-layouts, on_device(): mine = lax.slice_in_dim(image, start, start + rows, axis=1)  25.9 us
    dot_general x1, matrix products, on_device(): jnp.dot(image.reshape(chan_count * row_count, width_len), fwd_cols, prefe...  22.8 us
  transfers between devices with their start and end apart: 24, of which 11 were waited for; matrix products, arithmetic and copies ran while one was open for 10% of the time, Pallas kernels for 20%

profile of v1, /device:TPU:0, one launch (start us, length us, event | category | flops | bytes accessed | tf_op | source)
XLA Modules:
  0.0 844.0 jit_solution(14122057060660467722)
XLA Ops:
  6.5 17.8 %negate_convert_fusion.1 = (bf16[4096,256]{1,0:T(8,128)(2,1)S(1)}, bf16[4096,256]{1,0:T(8,128)(2,1)}) fusion(), kind=kLoop, calls=%fused_computation.34 | loop fusion | flops 17825792 | bytes 4194304 | tf_op jit(solution)/shard_map/convert.7
  24.4 3.1 slice.66
  27.5 2.5 cosine_convert_fusion.2
  30.0 22.8 %multiply_convert_fusion = bf16[4096,512]{1,0:T(8,128)(2,1)S(1)} fusion(bf16[4096,4096]{1,0:T(8,128)(2,1)} %bitcast.56, bf16[4096,256]{1,0:T(8,128)(2,1)S(1)} %get-tuple-element.124, bf16[4096,256]{1,0:T(8,128)(2,1)} %get-tuple-element.125), kind=kOutput, calls=%fused_computation.10 | convolution fusion | flops 17192452096 | bytes 41943040 | tf_op jit(solution)/shard_map/dot_general | solution.py:169
  58.2 5.6 copy.28
  64.0 17.5 %fusion.51 = (bf16[8,64,4096]{2,1,0:T(8,128)(2,1)}, bf16[8,64,4096]{2,1,0:T(8,128)(2,1)}, bf16[8,64,4096]{2,1,0:T(8,128)(2,1)}, bf16[8,64,4096]{2,1,0:T(8,128)(2...) fusion(bf16[8,512,4096]{2,1,0:T(8,128)(2,1)} %one_ref.9), kind=kLoop, calls=%fused_computation.103 | loop fusion | bytes 50331648 | tf_op jit(solution)/shard_map/slice | solution.py:142
  83.9 5.2 collective-permute-done.4.two_ref
  89.2 8.4 shard_map.50
  99.6 2.9 collective-permute-start.5
  102.5 52.1 %reduce-scatter.2.cloned.1.call-done = f32[8,32,512]{2,0,1:T(8,128)} async-done(((f32[8,256,512]{2,0,1:T(8,128)}), f32[8,32,512]{2,0,1:T(8,128)}) %reduce-scatter.2.cloned.1.call-update) | async-done | bytes 524304 | tf_op jit(solution)/shard_map/reduce_scatter | solution.py:185
  157.1 8.4 shard_map.51
  167.6 76.7 %collective-permute-done.9.one_ref = bf16[8,32,4096]{2,1,0:T(8,128)(2,1)} collective-permute-done((bf16[8,32,4096]{2,1,0:T(8,128)(2,1)}, bf16[8,32,4096]{2,1,0:T(8,128)(2,1)}, u32[]{:S(2)}, u32[]{:S(2)}) %collective-permute-start.9) | collective-permute-done | bytes 2097184 | tf_op jit(solution)/shard_map/ppermute | solution.py:138
  246.0 8.3 shard_map.49
  259.4 6.4 fusion
  267.5 16.9 %negate_convert_fusion = (bf16[256,4096]{1,0:T(8,128)(2,1)S(1)}, bf16[256,4096]{1,0:T(8,128)(2,1)S(1)}) fusion(), kind=kLoop, calls=%fused_computation.30 | loop fusion | flops 17825792 | bytes 4194304 | tf_op jit(solution)/shard_map/convert.1
  284.5 2.4 maximum_multiply_fusion.2.cols_ref
  288.5 3.3 shard_map.53.home_ref
  292.3 8.3 shard_map.52
  300.7 37.2 %collective-permute-done.10.came_ref = bf16[8,64,4096]{2,1,0:T(8,128)(2,1)} collective-permute-done((bf16[8,64,4096]{2,1,0:T(8,128)(2,1)}, bf16[8,64,4096]{2,1,0:T(8,128)(2,1)}, u32[]{:S(2)}, u32[]{:S(2)}) %collective-permute-start.10) | collective-permute-done | bytes 4194336 | tf_op jit(solution)/shard_map/ppermute | solution.py:234
  339.7 3.6 shard_map.54.came_ref
  344.6 8.4 shard_map.48
  355.0 72.8 %collective-permute-done.6.came_ref = bf16[8,64,4096]{2,1,0:T(8,128)(2,1)} collective-permute-done((bf16[8,64,4096]{2,1,0:T(8,128)(2,1)}, bf16[8,64,4096]{2,1,0:T(8,128)(2,1)}, u32[]{:S(2)}, u32[]{:S(2)}) %collective-permute-start.6) | collective-permute-done | bytes 4194336 | tf_op jit(solution)/shard_map/ppermute | solution.py:234
  427.8 7.2 convolution_bitcast_fusion.2
  435.1 5.5 convolution_bitcast_fusion.1
  440.6 10.4 %slice_subtract_fusion = (f32[8,512,256]{2,1,0:T(8,128)}, f32[8,512,256]{2,1,0:T(8,128)}) fusion(f32[8,512,512]{2,1,0:T(8,128)} %convolution_bitcast_fusion.1, f32[8,512,512]{2,1,0:T(8,128)} %convolution_bitcast_fusion.2), kind=kLoop, calls=%fused_computation.24 | loop fusion | flops 2097152 | bytes 25165824 | tf_op jit(solution)/shard_map/sub | solution.py:204
  451.0 5.5 fusion.4.back_ref
  456.5 7.2 shard_map.55.rest_0_
  463.7 11.8 %shard_map.56.rest_0_ = bf16[8,512,4096]{2,1,0:T(8,128)(2,1)} custom-call(f32[8,1]{1,0:T(8,128)S(1)} %copy.41.bias_ref, bf16[8,512,512]{2,1,0:T(8,128)(2,1)S(1)} %copy-done, bf16[512,4096]{1,0:T(8,128)(2,1)} %maximum_multiply_fusion.2.cols_ref, bf16[8,64,4096]{2,1,0:T(8,128)(2,1)} %copy-done.3, ...), custom_call_target="tpu_custom_call", output_to_operand_aliasing={{}: (5, {})} | custom-call | flops 2147483648 | bytes 12582912 | tf_op jit(solution)/shard_map/pallas_call | solution.py:112
  475.5 11.8 %shard_map.57.rest_0_ = bf16[8,512,4096]{2,1,0:T(8,128)(2,1)} custom-call(f32[8,1]{1,0:T(8,128)S(1)} %copy.41.bias_ref, bf16[8,512,512]{2,1,0:T(8,128)(2,1)S(1)} %copy-done, bf16[512,4096]{1,0:T(8,128)(2,1)} %maximum_multiply_fusion.2.cols_ref, bf16[8,64,4096]{2,1,0:T(8,128)(2,1)} %copy-done.5, ...), custom_call_target="tpu_custom_call", output_to_operand_aliasing={{}: (5, {})} | custom-call | flops 2147483648 | bytes 12582912 | tf_op jit(solution)/shard_map/pallas_call | solution.py:112
  489.1 4.0 slice.80
  493.1 7.3 shard_map.58
  502.3 15.4 %collective-permute-done.15.came_ref = bf16[8,64,4096]{2,1,0:T(8,128)(2,1)} collective-permute-done((bf16[8,64,4096]{2,1,0:T(8,128)(2,1)}, bf16[8,64,4096]{2,1,0:T(8,128)(2,1)}, u32[]{:S(2)}, u32[]{:S(2)}) %collective-permute-start.15) | collective-permute-done | bytes 4194336 | tf_op jit(solution)/shard_map/ppermute | solution.py:234
  517.7 11.8 %shard_map.59.rest_0_ = bf16[8,512,4096]{2,1,0:T(8,128)(2,1)} custom-call(f32[8,1]{1,0:T(8,128)S(1)} %copy.41.bias_ref, bf16[8,512,512]{2,1,0:T(8,128)(2,1)S(1)} %copy-done, bf16[512,4096]{1,0:T(8,128)(2,1)} %maximum_multiply_fusion.2.cols_ref, bf16[8,64,4096]{2,1,0:T(8,128)(2,1)} %copy-done.4, ...), custom_call_target="tpu_custom_call", output_to_operand_aliasing={{}: (5, {})} | custom-call | flops 2147483648 | bytes 12582912 | tf_op jit(solution)/shard_map/pallas_call | solution.py:112
  531.3 3.1 slice.87
  534.4 6.3 shard_map.47
  540.7 11.8 %shard_map.60.rest_0_ = bf16[8,512,4096]{2,1,0:T(8,128)(2,1)} custom-call(f32[8,1]{1,0:T(8,128)S(1)} %copy.41.bias_ref, bf16[8,512,512]{2,1,0:T(8,128)(2,1)S(1)} %copy-done, bf16[512,4096]{1,0:T(8,128)(2,1)} %maximum_multiply_fusion.2.cols_ref, bf16[8,64,4096]{2,1,0:T(8,128)(2,1)} %copy-done.7, ...), custom_call_target="tpu_custom_call", output_to_operand_aliasing={{}: (5, {})} | custom-call | flops 2147483648 | bytes 12582912 | tf_op jit(solution)/shard_map/pallas_call | solution.py:112
  552.5 55.1 %collective-permute-done.13.came_ref = bf16[8,64,4096]{2,1,0:T(8,128)(2,1)} collective-permute-done((bf16[8,64,4096]{2,1,0:T(8,128)(2,1)}, bf16[8,64,4096]{2,1,0:T(8,128)(2,1)}, u32[]{:S(2)}, u32[]{:S(2)}) %collective-permute-start.13) | collective-permute-done | bytes 4194336 | tf_op jit(solution)/shard_map/ppermute | solution.py:234
  613.6 4.0 shard_map.61
  618.9 78.5 %collective-permute-done.18.came_ref = bf16[8,64,4096]{2,1,0:T(8,128)(2,1)} collective-permute-done((bf16[8,64,4096]{2,1,0:T(8,128)(2,1)}, bf16[8,64,4096]{2,1,0:T(8,128)(2,1)}, u32[]{:S(2)}, u32[]{:S(2)}) %collective-permute-start.18) | collective-permute-done | bytes 4194336 | tf_op jit(solution)/shard_map/ppermute | solution.py:234
  697.5 11.8 %shard_map.62.rest_0_ = bf16[8,512,4096]{2,1,0:T(8,128)(2,1)} custom-call(f32[8,1]{1,0:T(8,128)S(1)} %copy.41.bias_ref, bf16[8,512,512]{2,1,0:T(8,128)(2,1)S(1)} %copy-done, bf16[512,4096]{1,0:T(8,128)(2,1)} %maximum_multiply_fusion.2.cols_ref, bf16[8,64,4096]{2,1,0:T(8,128)(2,1)} %copy-done.6, ...), custom_call_target="tpu_custom_call", output_to_operand_aliasing={{}: (5, {})} | custom-call | flops 2147483648 | bytes 12582912 | tf_op jit(solution)/shard_map/pallas_call | solution.py:112
  711.1 2.5 shard_map.46
  713.6 11.9 %shard_map.63.rest_0_ = bf16[8,512,4096]{2,1,0:T(8,128)(2,1)} custom-call(f32[8,1]{1,0:T(8,128)S(1)} %copy.41.bias_ref, bf16[8,512,512]{2,1,0:T(8,128)(2,1)S(1)} %copy-done, bf16[512,4096]{1,0:T(8,128)(2,1)} %maximum_multiply_fusion.2.cols_ref, bf16[8,64,4096]{2,1,0:T(8,128)(2,1)} %copy-done.8, ...), custom_call_target="tpu_custom_call", output_to_operand_aliasing={{}: (5, {})} | custom-call | flops 2147483648 | bytes 12582912 | tf_op jit(solution)/shard_map/pallas_call | solution.py:112
  725.4 39.5 %collective-permute-done.16.came_ref = bf16[8,48,4096]{2,1,0:T(8,128)(2,1)} collective-permute-done((bf16[8,48,4096]{2,1,0:T(8,128)(2,1)}, bf16[8,48,4096]{2,1,0:T(8,128)(2,1)}, u32[]{:S(2)}, u32[]{:S(2)}) %collective-permute-start.16) | collective-permute-done | bytes 3145760 | tf_op jit(solution)/shard_map/ppermute | solution.py:234
  766.6 11.1 %shard_map.64.rest_0_ = bf16[8,512,4096]{2,1,0:T(8,128)(2,1)} custom-call(f32[8,1]{1,0:T(8,128)S(1)} %copy.41.bias_ref, bf16[8,512,512]{2,1,0:T(8,128)(2,1)} %fusion.4.back_ref, bf16[512,4096]{1,0:T(8,128)(2,1)} %maximum_multiply_fusion.2.cols_ref, bf16[8,48,4096]{2,1,0:T(8,128)(2,1)S(1)} %get-tuple-element.92.home_ref, ...), custom_call_target="tpu_custom_call", output_to_operand_aliasing={{}: (5, {})} | custom-call | flops 1610612736 | bytes 9437184 | tf_op jit(solution)/shard_map/pallas_call | solution.py:112
  777.7 32.0 %collective-permute-done.20.came_ref = bf16[8,32,4096]{2,1,0:T(8,128)(2,1)S(1)} collective-permute-done((bf16[8,32,4096]{2,1,0:T(8,128)(2,1)}, bf16[8,32,4096]{2,1,0:T(8,128)(2,1)S(1)}, u32[]{:S(2)}, u32[]{:S(2)}) %collective-permute-start.20) | collective-permute-done | bytes 2097184 | tf_op jit(solution)/shard_map/ppermute | solution.py:234
  812.7 8.2 shard_map.65.rest_0_
  820.9 10.9 %collective-permute-done.19.came_ref = bf16[8,16,4096]{2,1,0:T(8,128)(2,1)S(1)} collective-permute-done((bf16[8,16,4096]{2,1,0:T(8,128)(2,1)S(1)}, bf16[8,16,4096]{2,1,0:T(8,128)(2,1)S(1)}, u32[]{:S(2)}, u32[]{:S(2)}) %collective-permute-start.19) | collective-permute-done | bytes 1048608 | tf_op jit(solution)/shard_map/ppermute | solution.py:234
  831.8 5.7 shard_map.66
  (104 shorter events, 49.5 us)
Async XLA Ops:
  6.5 148.0 %reduce-scatter.2.cloned.1.call-start = ((), (), s32[]{:S(2)}) async-start(), calls=%async_computation.1 | async-start | bytes 4718592 | tf_op jit(solution)/shard_map/reduce_scatter | solution.py:185
  63.8 18.8 %copy-start.18 = (bf16[32,32]{1,0:T(8,128)(2,1)S(1)}, bf16[32,32]{1,0:T(8,128)(2,1)}, u32[]{:S(2)}) copy-start(bf16[32,32]{1,0:T(8,128)(2,1)} %param.6) | copy-start | bytes 6148
  63.8 192.9 %all-gather.3.cloned.1.call-start = ((), (), s32[]{:S(2)}) async-start(), calls=%async_computation.2 | async-start | bytes 1310720 | tf_op jit(solution)/shard_map/all_gather | solution.py:187
  81.5 7.6 collective-permute-start.4
  82.0 162.2 %collective-permute-start.3 = (bf16[8,64,4096]{2,1,0:T(8,128)(2,1)}, bf16[8,64,4096]{2,1,0:T(8,128)(2,1)}, u32[]{:S(2)}, u32[]{:S(2)}) collective-permute-start(bf16[8,64,4096]{2,1,0:T(8,128)(2,1)} %get-tuple-element.105), channel_id=1, source_target_pairs={{0,1},{1,0},{2,3},{3,2},{4,5},{5,4},{6,7},{7,6},{8,9},{9,8},{10,11... | collective-permute-start | bytes 12582920 | tf_op jit(solution)/shard_map/ppermute | solution.py:143
  82.1 74.5 %collective-permute-start.7 = (bf16[8,64,4096]{2,1,0:T(8,128)(2,1)}, bf16[8,64,4096]{2,1,0:T(8,128)(2,1)}, u32[]{:S(2)}, u32[]{:S(2)}) collective-permute-start(bf16[8,64,4096]{2,1,0:T(8,128)(2,1)} %get-tuple-element.103), channel_id=1, source_target_pairs={{0,1},{1,0},{2,3},{3,2},{4,5},{5,4},{6,7},{7,6},{8,9},{9,8},{10,11... | collective-permute-start | bytes 12582920 | tf_op jit(solution)/shard_map/ppermute | solution.py:143
  97.6 2.0 copy-start.3
  99.6 156.9 %collective-permute-start.5 = (bf16[8,64,4096]{2,1,0:T(8,128)(2,1)}, bf16[8,64,4096]{2,1,0:T(8,128)(2,1)}, u32[]{:S(2)}, u32[]{:S(2)}) collective-permute-start(bf16[8,64,4096]{2,1,0:T(8,128)(2,1)} %get-tuple-element.56), channel_id=1, source_target_pairs={{0,2},{1,3},{2,0},{3,1},{4,6},{5,7},{6,4},{7,5},{8,10},{9,11},{10,... | collective-permute-start | bytes 12582920 | tf_op jit(solution)/shard_map/ppermute | solution.py:234
  102.4 141.8 %collective-permute-start.9 = (bf16[8,32,4096]{2,1,0:T(8,128)(2,1)}, bf16[8,32,4096]{2,1,0:T(8,128)(2,1)}, u32[]{:S(2)}, u32[]{:S(2)}) collective-permute-start(bf16[8,32,4096]{2,1,0:T(8,128)(2,1)} %slice.66), channel_id=1, source_target_pairs={{0,2},{1,3},{2,0},{3,1},{4,6},{5,7},{6,4},{7,5},{8,10},{9,11},{10,... | collective-permute-start | bytes 6291464 | tf_op jit(solution)/shard_map/ppermute | solution.py:138
  156.4 271.4 %all-gather.5.cloned.1.call-start = ((), (), s32[]{:S(2)}) async-start(), calls=%async_computation.3 | async-start | bytes 2359296 | tf_op jit(solution)/shard_map/all_gather | solution.py:199
  156.5 110.4 %collective-permute-start.11 = (bf16[8,32,4096]{2,1,0:T(8,128)(2,1)}, bf16[8,32,4096]{2,1,0:T(8,128)(2,1)S(1)}, u32[]{:S(2)}, u32[]{:S(2)}) collective-permute-start(bf16[8,32,4096]{2,1,0:T(8,128)(2,1)} %slice.66), channel_id=1, source_target_pairs={{0,1},{1,0},{2,3},{3,2},{4,5},{5,4},{6,7},{7,6},{8,9},{9,8},{10,11... | collective-permute-start | bytes 6291464 | tf_op jit(solution)/shard_map/ppermute | solution.py:140
  156.6 135.2 %collective-permute-start.8 = (bf16[8,64,4096]{2,1,0:T(8,128)(2,1)}, bf16[8,64,4096]{2,1,0:T(8,128)(2,1)}, u32[]{:S(2)}, u32[]{:S(2)}) collective-permute-start(bf16[8,64,4096]{2,1,0:T(8,128)(2,1)} %get-tuple-element.102), channel_id=1, source_target_pairs={{0,1},{1,0},{2,3},{3,2},{4,5},{5,4},{6,7},{7,6},{8,9},{9,8},{10,11... | collective-permute-start | bytes 12582920 | tf_op jit(solution)/shard_map/ppermute | solution.py:143
  165.5 2.1 copy-start.5
  244.2 100.4 %collective-permute-start.2 = (bf16[8,64,4096]{2,1,0:T(8,128)(2,1)}, bf16[8,64,4096]{2,1,0:T(8,128)(2,1)}, u32[]{:S(2)}, u32[]{:S(2)}) collective-permute-start(bf16[8,64,4096]{2,1,0:T(8,128)(2,1)} %get-tuple-element.106), channel_id=1, source_target_pairs={{0,1},{1,0},{2,3},{3,2},{4,5},{5,4},{6,7},{7,6},{8,9},{9,8},{10,11... | collective-permute-start | bytes 12582920 | tf_op jit(solution)/shard_map/ppermute | solution.py:143
  244.2 93.7 %collective-permute-start.10 = (bf16[8,64,4096]{2,1,0:T(8,128)(2,1)}, bf16[8,64,4096]{2,1,0:T(8,128)(2,1)}, u32[]{:S(2)}, u32[]{:S(2)}) collective-permute-start(bf16[8,64,4096]{2,1,0:T(8,128)(2,1)} %get-tuple-element.62), channel_id=1, source_target_pairs={{0,2},{1,3},{2,0},{3,1},{4,6},{5,7},{6,4},{7,5},{8,10},{9,11},{10,... | collective-permute-start | bytes 12582920 | tf_op jit(solution)/shard_map/ppermute | solution.py:234
  254.3 2.1 copy-start.4
  256.4 171.4 %collective-permute-start.6 = (bf16[8,64,4096]{2,1,0:T(8,128)(2,1)}, bf16[8,64,4096]{2,1,0:T(8,128)(2,1)}, u32[]{:S(2)}, u32[]{:S(2)}) collective-permute-start(bf16[8,64,4096]{2,1,0:T(8,128)(2,1)} %get-tuple-element.57), channel_id=1, source_target_pairs={{0,2},{1,3},{2,0},{3,1},{4,6},{5,7},{6,4},{7,5},{8,10},{9,11},{10,... | collective-permute-start | bytes 12582920 | tf_op jit(solution)/shard_map/ppermute | solution.py:234
  259.4 8.0 copy-start.19
  266.9 17.6 %copy-start.9 = (bf16[8,32,4096]{2,1,0:T(8,128)(2,1)}, bf16[8,32,4096]{2,1,0:T(8,128)(2,1)S(1)}, u32[]{:S(2)}) copy-start(bf16[8,32,4096]{2,1,0:T(8,128)(2,1)S(1)} %collective-permute-done.11.two_ref) | copy-start | bytes 6291460
  266.9 72.8 %collective-permute-start.12 = (bf16[8,32,4096]{2,1,0:T(8,128)(2,1)}, bf16[8,32,4096]{2,1,0:T(8,128)(2,1)}, u32[]{:S(2)}, u32[]{:S(2)}) collective-permute-start(bf16[8,32,4096]{2,1,0:T(8,128)(2,1)} %collective-permute-done.9.one_ref), channel_id=1, source_target_pairs={{0,1},{1,0},{2,3},{3,2},{4,5},{5,4},{6,7},{7,6},{8,9},{9,8},{10,11... | collective-permute-start | bytes 6291464 | tf_op jit(solution)/shard_map/ppermute | solution.py:218
  286.9 1.6 copy-start.10
  291.8 201.3 %collective-permute-start.14 = (bf16[8,64,4096]{2,1,0:T(8,128)(2,1)}, bf16[8,64,4096]{2,1,0:T(8,128)(2,1)}, u32[]{:S(2)}, u32[]{:S(2)}) collective-permute-start(bf16[8,64,4096]{2,1,0:T(8,128)(2,1)} %get-tuple-element.101), channel_id=1, source_target_pairs={{0,1},{1,0},{2,3},{3,2},{4,5},{5,4},{6,7},{7,6},{8,9},{9,8},{10,11... | collective-permute-start | bytes 12582920 | tf_op jit(solution)/shard_map/ppermute | solution.py:143
  300.7 42.6 %copy-start.7 = (bf16[8,64,4096]{2,1,0:T(8,128)(2,1)}, bf16[8,64,4096]{2,1,0:T(8,128)(2,1)S(1)}, u32[]{:S(2)}) copy-start(bf16[8,64,4096]{2,1,0:T(8,128)(2,1)S(1)} %get-tuple-element.69.home_ref) | copy-start | bytes 12582916
  337.9 179.8 %collective-permute-start.15 = (bf16[8,64,4096]{2,1,0:T(8,128)(2,1)}, bf16[8,64,4096]{2,1,0:T(8,128)(2,1)}, u32[]{:S(2)}, u32[]{:S(2)}) collective-permute-start(bf16[8,64,4096]{2,1,0:T(8,128)(2,1)} %get-tuple-element.71), channel_id=1, source_target_pairs={{0,2},{1,3},{2,0},{3,1},{4,6},{5,7},{6,4},{7,5},{8,10},{9,11},{10,... | collective-permute-start | bytes 12582920 | tf_op jit(solution)/shard_map/ppermute | solution.py:234
  343.3 1.3 copy-start.1
  353.0 2.0 copy-start.6
  427.8 7.2 copy-start.17
  451.0 5.5 copy-start.2
  456.5 7.2 copy-start
  487.4 120.2 %collective-permute-start.13 = (bf16[8,64,4096]{2,1,0:T(8,128)(2,1)}, bf16[8,64,4096]{2,1,0:T(8,128)(2,1)}, u32[]{:S(2)}, u32[]{:S(2)}) collective-permute-start(bf16[8,64,4096]{2,1,0:T(8,128)(2,1)} %get-tuple-element.67), channel_id=1, source_target_pairs={{0,2},{1,3},{2,0},{3,1},{4,6},{5,7},{6,4},{7,5},{8,10},{9,11},{10,... | collective-permute-start | bytes 12582920 | tf_op jit(solution)/shard_map/ppermute | solution.py:234
  493.1 41.3 %collective-permute-start.1 = (bf16[8,48,4096]{2,1,0:T(8,128)(2,1)}, bf16[8,48,4096]{2,1,0:T(8,128)(2,1)S(1)}, u32[]{:S(2)}, u32[]{:S(2)}) collective-permute-start(bf16[8,48,4096]{2,1,0:T(8,128)(2,1)} %slice.80), channel_id=1, source_target_pairs={{0,1},{1,0},{2,3},{3,2},{4,5},{5,4},{6,7},{7,6},{8,9},{9,8},{10,11... | collective-permute-start | bytes 9437192 | tf_op jit(solution)/shard_map/ppermute | solution.py:143
  500.4 2.0 copy-start.15
  502.3 27.2 %copy-start.8 = (bf16[8,64,4096]{2,1,0:T(8,128)(2,1)}, bf16[8,64,4096]{2,1,0:T(8,128)(2,1)S(1)}, u32[]{:S(2)}) copy-start(bf16[8,64,4096]{2,1,0:T(8,128)(2,1)S(1)} %get-tuple-element.80.home_ref) | copy-start | bytes 12582916
  529.5 167.9 %collective-permute-start.18 = (bf16[8,64,4096]{2,1,0:T(8,128)(2,1)}, bf16[8,64,4096]{2,1,0:T(8,128)(2,1)}, u32[]{:S(2)}, u32[]{:S(2)}) collective-permute-start(bf16[8,64,4096]{2,1,0:T(8,128)(2,1)} %copy-done.15), channel_id=1, source_target_pairs={{0,2},{1,3},{2,0},{3,1},{4,6},{5,7},{6,4},{7,5},{8,10},{9,11},{10,... | collective-permute-start | bytes 12582920 | tf_op jit(solution)/shard_map/ppermute | solution.py:234
  534.4 76.3 %collective-permute-start.17 = (bf16[8,32,4096]{2,1,0:T(8,128)(2,1)}, bf16[8,32,4096]{2,1,0:T(8,128)(2,1)S(1)}, u32[]{:S(2)}, u32[]{:S(2)}) collective-permute-start(bf16[8,32,4096]{2,1,0:T(8,128)(2,1)} %slice.87), channel_id=1, source_target_pairs={{0,1},{1,0},{2,3},{3,2},{4,5},{5,4},{6,7},{7,6},{8,9},{9,8},{10,11... | collective-permute-start | bytes 6291464 | tf_op jit(solution)/shard_map/ppermute | solution.py:143
  607.6 157.3 %collective-permute-start.16 = (bf16[8,48,4096]{2,1,0:T(8,128)(2,1)}, bf16[8,48,4096]{2,1,0:T(8,128)(2,1)}, u32[]{:S(2)}, u32[]{:S(2)}) collective-permute-start(bf16[8,48,4096]{2,1,0:T(8,128)(2,1)} %get-tuple-element.78), channel_id=1, source_target_pairs={{0,2},{1,3},{2,0},{3,1},{4,6},{5,7},{6,4},{7,5},{8,10},{9,11},{10,... | collective-permute-start | bytes 9437192 | tf_op jit(solution)/shard_map/ppermute | solution.py:234
  610.6 100.4 %collective-permute-start = (bf16[8,16,4096]{2,1,0:T(8,128)(2,1)S(1)}, bf16[8,16,4096]{2,1,0:T(8,128)(2,1)S(1)}, u32[]{:S(2)}, u32[]{:S(2)}) collective-permute-start(bf16[8,16,4096]{2,1,0:T(8,128)(2,1)S(1)} %slice.79), channel_id=1, source_target_pairs={{0,1},{1,0},{2,3},{3,2},{4,5},{5,4},{6,7},{7,6},{8,9},{9,8},{10,11... | collective-permute-start | bytes 3145736 | tf_op jit(solution)/shard_map/ppermute | solution.py:143
  610.7 1.3 copy-start.13
  612.0 1.6 copy-start.14
  617.6 1.3 copy-start.16
  709.3 100.4 %collective-permute-start.20 = (bf16[8,32,4096]{2,1,0:T(8,128)(2,1)}, bf16[8,32,4096]{2,1,0:T(8,128)(2,1)S(1)}, u32[]{:S(2)}, u32[]{:S(2)}) collective-permute-start(bf16[8,32,4096]{2,1,0:T(8,128)(2,1)} %copy-done.16), channel_id=1, source_target_pairs={{0,2},{1,3},{2,0},{3,1},{4,6},{5,7},{6,4},{7,5},{8,10},{9,11},{10,... | collective-permute-start | bytes 6291464 | tf_op jit(solution)/shard_map/ppermute | solution.py:234
  764.9 66.9 %collective-permute-start.19 = (bf16[8,16,4096]{2,1,0:T(8,128)(2,1)S(1)}, bf16[8,16,4096]{2,1,0:T(8,128)(2,1)S(1)}, u32[]{:S(2)}, u32[]{:S(2)}) collective-permute-start(bf16[8,16,4096]{2,1,0:T(8,128)(2,1)S(1)} %get-tuple-element.89), channel_id=1, source_target_pairs={{0,2},{1,3},{2,0},{3,1},{4,6},{5,7},{6,4},{7,5},{8,10},{9,11},{10,... | collective-permute-start | bytes 3145736 | tf_op jit(solution)/shard_map/ppermute | solution.py:234
  809.7 1.4 copy-start.11
  811.1 1.6 copy-start.12
Sparse Core Ops, SparseCore 0:
  63.9 90.5 reduce-scatter.1
  156.6 22.2 all-gather.2
  267.0 50.9 all-gather.4

commit v2 on v1

--- a/solution.py
+++ b/solution.py
@@ -10,7 +10,7 @@
 MX = 256
 MY = 256
 UNIT = 16
-SLACK = 5
+SLACK = 9
 
 
 def wave_table(points, freqs, length):
@@ -20,9 +20,9 @@
 
 
 def chunk_rows(row_count):
-    if row_count >= 512:
-        middle, rest = divmod(row_count - 128, 64)
-        sizes = [32] + [64] * middle + [48, 32, 16] + [UNIT] * (rest // UNIT)
+    if row_count >= 256:
+        middle, rest = divmod(row_count - 192, 64)
+        sizes = [32, 32, 32] + [64] * middle + [48, 32, 16] + [UNIT] * (rest // UNIT)
     else:
         sizes = [UNIT] * (row_count // UNIT)
     starts = [sum(sizes[:n]) for n in range(len(sizes))]
@@ -134,13 +134,13 @@
     core_swap = [(c, c ^ 1) for c in range(chan_devs)]
     chip_swap = [(c, c ^ 2) for c in range(chan_devs)]
     chunks = chunk_rows(row_count)
+    def swap(part, start, rows):
+        mine = lax.slice_in_dim(part, start, start + rows, axis=1)
+        return lax.ppermute(mine, "chan", core_swap)
+
     first_mine = lax.slice_in_dim(image, 0, chunks[0][1], axis=1)
     first_far = lax.ppermute(first_mine, "chan", chip_swap)
     first_mine, image = lax.optimization_barrier((first_mine, image))
-    peers = [lax.ppermute(first_mine, "chan", core_swap)]
-    for start, rows in chunks[1:]:
-        mine = lax.slice_in_dim(image, start, start + rows, axis=1)
-        peers.append(lax.ppermute(mine, "chan", core_swap))
 
     def kron(out_dev, in_dev):
         eye = jnp.eye(UNIT, dtype=jnp.bfloat16)
@@ -158,8 +158,56 @@
     kron_far = kron(chan_index, chan_index ^ 2)
     kron_both = jnp.concatenate([kron(chan_index ^ 2, chan_index), kron_home], 0)
 
+    cames = {}
+    homes = {}
+    done = []
+
+    peers = {}
+
+    def meet(n):
+        if n < len(chunks):
+            peers[n] = swap(image, *chunks[n])
+
+    def issue(n):
+        if n >= len(chunks):
+            return
+        peer = peers[n]
+        away, homes[n] = partials(image, peer, kron_both, *chunks[n])
+        before = 3 * (n - SLACK) + 4
+        if n >= SLACK:
+            finish_until(before)
+            away, done[before - 1] = lax.optimization_barrier((away, done[before - 1]))
+        cames[n] = lax.ppermute(away, "chan", chip_swap)
+
+    def gate(n, *values):
+        if n + 1 >= len(chunks):
+            return values
+        cames[n], homes[n + 1], *values = lax.optimization_barrier(
+            (cames[n], homes[n + 1], *values)
+        )
+        return values
+
+    def finish_until(count):
+        while len(done) < count:
+            n = len(done)
+            last = done[-1] if done else None
+            done.append(
+                finish(bias, rowback, back_cols, homes[n], cames[n], chunks[n][0], last)
+            )
+
+    meet(1)
+    meet(2)
+    issue(1)
+    issue(2)
+    col_pts = jnp.arange(width_len, dtype=jnp.int32)
     row_global = row_index * row_count + jnp.arange(row_count, dtype=jnp.int32)
-    col_pts = jnp.arange(width_len, dtype=jnp.int32)
+    bias = bias[:, None]
+    first_far, first_mine, image, col_pts = gate(1, first_far, first_mine, image, col_pts)
+    meet(3)
+    meet(4)
+    issue(3)
+    image, row_global = gate(2, image, row_global)
+
     col_freq = jnp.arange(MY, dtype=jnp.int32)
     cos_w, sin_w = wave_table(col_pts, col_freq, width_len)
     fwd_cols = jnp.concatenate([cos_w, -sin_w], 1).astype(jnp.bfloat16)
@@ -176,6 +224,11 @@
         .astype(jnp.bfloat16)
         .reshape(chan_count, row_count, 2 * MY)
     )
+    meet(5)
+    issue(4)
+    image, colspec = gate(3, image, colspec)
+    meet(6)
+    issue(5)
     cos_h, sin_h = wave_table(row_global, row_freq, full_rows)
     fwd_rows = jnp.concatenate([cos_h, sin_h], 1).astype(jnp.bfloat16)
     partial_value = jnp.einsum("chp,hq->cqp", colspec, fwd_rows, preferred_element_type=jnp.float32)
@@ -183,6 +236,12 @@
     spec_im = partial_value[:, :MX, MY:] - partial_value[:, MX:, :MY]
     partial_value = jnp.concatenate([spec_re, spec_im], -1) * (1.0 / math.sqrt(full_rows))
     block = lax.psum_scatter(partial_value, "row", scatter_dimension=1, tiled=True)
+    (image,) = gate(4, image)
+    meet(7)
+    issue(6)
+    image, block = gate(5, image, block)
+    meet(8)
+    issue(7)
     spectrum = block.astype(jnp.bfloat16)
     all_inputs = lax.all_gather(spectrum, "chan", axis=0, tiled=True)
     zed_re = all_inputs[..., :MY].astype(jnp.float32)
@@ -197,6 +256,9 @@
     )
     mixed = jnp.concatenate([mix_re, mix_im], -1).astype(jnp.bfloat16)
     piece = lax.all_gather(mixed, "row", axis=1, tiled=True)
+    image, piece = gate(6, image, piece)
+    meet(9)
+    issue(8)
     cos_back = cos_h.T.astype(jnp.bfloat16)
     sin_back = sin_h.T.astype(jnp.bfloat16)
     with_cos = jnp.einsum("okp,kh->ohp", piece, cos_back, preferred_element_type=jnp.float32)
@@ -205,37 +267,16 @@
     back_im = with_sin[..., :MY] + with_cos[..., MY:]
     rowback = (jnp.concatenate([back_re, back_im], -1) * (1.0 / math.sqrt(MX))).astype(jnp.bfloat16)
 
-    bias = bias[:, None]
-    held = None
-    homes, cames = [], []
-    done = 0
-
-    def finish_next():
-        return finish(bias, rowback, back_cols, homes[done], cames[done], chunks[done][0], held)
-
-    for n, (start, rows) in enumerate(chunks):
-        if n == 0:
-            first_other = lax.ppermute(first_far, "chan", core_swap)
-            homes += partials(image, peers[0], kron_home, start, rows)
-            cames += partials(first_far, first_other, kron_far, 0, rows)
-            continue
-        away, home = partials(image, peers[n], kron_both, start, rows)
-        if n >= 2:
-            before = first_far if n == 2 else cames[n - 2]
-            away, before = lax.optimization_barrier((away, before))
-            if n > 2:
-                cames[n - 2] = before
-        if n >= SLACK:
-            while done <= n - 3:
-                held = finish_next()
-                done += 1
-            away, held = lax.optimization_barrier((away, held))
-        homes.append(home)
-        cames.append(lax.ppermute(away, "chan", chip_swap))
-    while done < len(chunks):
-        held = finish_next()
-        done += 1
-    return held
+    first_peer = lax.ppermute(first_mine, "chan", core_swap)
+    (homes[0],) = partials(image, first_peer, kron_home, *chunks[0])
+    first_other = lax.ppermute(first_far, "chan", core_swap)
+    (cames[0],) = partials(first_far, first_other, kron_far, 0, chunks[0][1])
+    for n in range(9, len(chunks)):
+        (image,) = gate(n - 2, image)
+        meet(n + 1)
+        issue(n)
+    finish_until(len(chunks))
+    return done[-1]
 
 
 def solution(mesh):

time: 845 us -> 801 us (0.948); the launches traced: 844 us -> 791 us
  waiting for transfers between devices: 475 us -> 412 us
    reduce_scatter x1, waiting for transfers between devices: 52.1 us -> 0.01 us  [on_device(): lax.psum_scatter(partial_value, 'row', scatter_dimension=1, tiled=True)]
    ppermute x1, waiting for transfers between devices: 76.7 us -> 31.5 us  [on_device(): first_far = lax.ppermute(first_mine, 'chan', chip_swap)]
    all_gather x1, waiting for transfers between devices: 0.01 us -> 22.2 us  [on_device(): all_inputs = lax.all_gather(spectrum, 'chan', axis=0, tiled=True)]
    ppermute x19 -> x21, waiting for transfers between devices: 347 us -> 358 us  [the longest x10 353 us: issue(): cames[n] = lax.ppermute(away, 'chan', chip_swap)]
    slice x4 -> x8, local copies, waits for them, and re-layouts: 25.9 us -> 33.3 us  [swap(): mine = lax.slice_in_dim(part, start, start + rows, axis=1)]
    unnamed x43 -> x51, local copies, waits for them, and re-layouts: 21.4 us -> 15.4 us
    pallas_call x10 -> x11, Pallas kernels: 103 us -> 107 us  [finish(): pl.pallas_call(final_kernel, grid=(rows // tall,), in_specs=in_specs, out...]
    ppermute x19 -> x21, starting transfers between devices: 17.6 us -> 14 us  [the longest x10 12.6 us: issue(): cames[n] = lax.ppermute(away, 'chan', chip_swap)]
  transfers between devices with their start and end apart: 24 -> 26, of which waited for: 11 -> 10; matrix products, arithmetic and copies ran while one was open for 10% -> 18% of each run, Pallas kernels for 20% -> 21%
where the time goes in v2:
time: 801 us; the launch traced here: 791 us
  waiting for transfers between devices  412 us (51%)
  Pallas kernels  175 us (22%)
  other arithmetic  71 us (9%)
  local copies, waits for them, and re-layouts  65.9 us (8%)
  matrix products  36.5 us (5%)
  starting transfers between devices  17.1 us (2%)
  between operations  13.9 us (2%)
    ppermute x10, waiting for transfers between devices, issue(): cames[n] = lax.ppermute(away, 'chan', chip_swap)  353 us
    pallas_call x11, Pallas kernels, finish(): pl.pallas_call(final_kernel, grid=(rows // tall,), in_specs=in_specs, out...  107 us
    pallas_call x12, Pallas kernels, partials(): pl.pallas_call(partial_kernel, grid=(rows // UNIT,), in_specs=[pl.BlockSp...  68.2 us
    another operation x3, other arithmetic  39.3 us
    slice x8, local copies, waits for them, and re-layouts, swap(): mine = lax.slice_in_dim(part, start, start + rows, axis=1)  33.3 us
    ppermute x1, waiting for transfers between devices, on_device(): first_far = lax.ppermute(first_mine, 'chan', chip_swap)  31.5 us
    dot_general x1, matrix products, on_device(): jnp.dot(image.reshape(chan_count * row_count, width_len), fwd_cols, prefe...  23 us
    all_gather x1, waiting for transfers between devices, on_device(): all_inputs = lax.all_gather(spectrum, 'chan', axis=0, tiled=True)  22.2 us
  transfers between devices with their start and end apart: 26, of which 10 were waited for; matrix products, arithmetic and copies ran while one was open for 18% of the time, Pallas kernels for 21%

profile of v2, /device:TPU:0, one launch (start us, length us, event | category | flops | bytes accessed | tf_op | source)
XLA Modules:
  0.0 791.4 jit_solution(13703547846449863656)
XLA Ops:
  6.5 3.2 slice.69
  9.7 4.7 fusion.52
  20.9 4.3 shard_map.47
  27.5 5.1 shard_map.46
  32.6 31.5 %collective-permute-done.4.one_ref = bf16[8,32,4096]{2,1,0:T(8,128)(2,1)S(1)} collective-permute-done((bf16[8,32,4096]{2,1,0:T(8,128)(2,1)}, bf16[8,32,4096]{2,1,0:T(8,128)(2,1)S(1)}, u32[]{:S(2)}, u32[]{:S(2)}) %collective-permute-start.4) | collective-permute-done | bytes 2097184 | tf_op jit(solution)/shard_map/ppermute | solution.py:142
  64.1 44.8 %collective-permute-done.3.came_ref = bf16[8,32,4096]{2,1,0:T(8,128)(2,1)S(1)} collective-permute-done((bf16[8,32,4096]{2,1,0:T(8,128)(2,1)S(1)}, bf16[8,32,4096]{2,1,0:T(8,128)(2,1)S(1)}, u32[]{:S(2)}, u32[]{:S(2)}) %collective-permute-start.3) | collective-permute-done | bytes 2097184 | tf_op jit(solution)/shard_map/ppermute | solution.py:180
  108.8 6.9 fusion.51
  118.1 5.2 collective-permute-done.5.two_ref
  123.3 7.3 shard_map.48
  132.4 19.7 %cosine_convert_fusion.1 = (bf16[4096,256]{1,0:T(8,128)(2,1)S(1)}, bf16[4096,256]{1,0:T(8,128)(2,1)}) fusion(s32[4096]{0:T(1024)S(1)} %iota.51), kind=kLoop, calls=%fused_computation.35 | loop fusion | flops 17825792 | bytes 4210688 | tf_op jit(solution)/shard_map/convert.8
  152.0 13.1 %collective-permute-done.1.came_ref = bf16[8,32,4096]{2,1,0:T(8,128)(2,1)} collective-permute-done((bf16[8,32,4096]{2,1,0:T(8,128)(2,1)}, bf16[8,32,4096]{2,1,0:T(8,128)(2,1)}, u32[]{:S(2)}, u32[]{:S(2)}) %collective-permute-start.1) | collective-permute-done | bytes 2097184 | tf_op jit(solution)/shard_map/ppermute | solution.py:180
  165.1 4.7 slice.74
  169.8 7.3 shard_map.49
  183.6 23.0 %multiply_convert_fusion = bf16[4096,512]{1,0:T(8,128)(2,1)S(1)} fusion(bf16[4096,4096]{1,0:T(8,128)(2,1)} %bitcast.56, bf16[4096,256]{1,0:T(8,128)(2,1)} %get-tuple-element.138, bf16[4096,256]{1,0:T(8,128)(2,1)S(1)} %get-tuple-element.137), kind=kOutput, calls=%fused_computation.10 | convolution fusion | flops 17192452096 | bytes 41943040 | tf_op jit(solution)/shard_map/dot_general | solution.py:217
  206.6 47.5 %collective-permute-done.8.came_ref = bf16[8,64,4096]{2,1,0:T(8,128)(2,1)} collective-permute-done((bf16[8,64,4096]{2,1,0:T(8,128)(2,1)S(1)}, bf16[8,64,4096]{2,1,0:T(8,128)(2,1)}, u32[]{:S(2)}, u32[]{:S(2)}) %collective-permute-start.8) | collective-permute-done | bytes 4194336 | tf_op jit(solution)/shard_map/ppermute | solution.py:180
  259.5 5.6 copy.30
  269.5 7.3 shard_map.50
  277.2 81.8 %collective-permute-done.7.came_ref = bf16[8,64,4096]{2,1,0:T(8,128)(2,1)S(1)} collective-permute-done((bf16[8,64,4096]{2,1,0:T(8,128)(2,1)}, bf16[8,64,4096]{2,1,0:T(8,128)(2,1)S(1)}, u32[]{:S(2)}, u32[]{:S(2)}) %collective-permute-start.7) | collective-permute-done | bytes 4194336 | tf_op jit(solution)/shard_map/ppermute | solution.py:180
  358.9 6.2 slice.80
  365.2 6.9 shard_map.51
  376.0 71.1 %collective-permute-done.12.came_ref = bf16[8,64,4096]{2,1,0:T(8,128)(2,1)} collective-permute-done((bf16[8,64,4096]{2,1,0:T(8,128)(2,1)S(1)}, bf16[8,64,4096]{2,1,0:T(8,128)(2,1)}, u32[]{:S(2)}, u32[]{:S(2)}) %collective-permute-start.12) | collective-permute-done | bytes 4194336 | tf_op jit(solution)/shard_map/ppermute | solution.py:180
  450.9 22.2 %all-gather.3.cloned.1.call-done = bf16[32,32,512]{2,1,0:T(8,128)(2,1)} async-done(((bf16[8,32,512]{2,1,0:T(8,128)(2,1)}), bf16[32,32,512]{2,1,0:T(8,128)(2,1)}) %all-gather.3.cloned.1.call-update) | async-done | bytes 1048592 | tf_op jit(solution)/shard_map/all_gather | solution.py:246
  475.8 6.6 fusion
  483.6 8.4 %shard_map.52 = (bf16[8,64,4096]{2,1,0:T(8,128)(2,1)}, bf16[8,64,4096]{2,1,0:T(8,128)(2,1)S(1)}) custom-call(bf16[8,512,4096]{2,1,0:T(8,128)(2,1)} %one_ref.10, bf16[8,64,4096]{2,1,0:T(8,128)(2,1)} %collective-permute-done.13.two_ref, bf16[256,256]{1,0:T(8,128)(2,1)S(1)} %constant_dynamic-update-slice_fusion.kron_ref), custom_call_target="tpu_custom_call" | custom-call | flops 2147483648 | bytes 16777216 | tf_op jit(solution)/shard_map/pallas_call | solution.py:55
  494.2 3.9 slice.89
  499.2 17.2 %cosine_convert_fusion = (bf16[256,4096]{1,0:T(8,128)(2,1)S(1)}, bf16[256,4096]{1,0:T(8,128)(2,1)S(1)}) fusion(s32[4096]{0:T(1024)S(1)} %iota.51), kind=kLoop, calls=%fused_computation.31 | loop fusion | flops 17825792 | bytes 4210688 | tf_op jit(solution)/shard_map/convert
  518.8 3.4 shard_map.57.came_ref
  522.1 26.4 %collective-permute-done.11.came_ref = bf16[8,64,4096]{2,1,0:T(8,128)(2,1)} collective-permute-done((bf16[8,64,4096]{2,1,0:T(8,128)(2,1)}, bf16[8,64,4096]{2,1,0:T(8,128)(2,1)}, u32[]{:S(2)}, u32[]{:S(2)}) %collective-permute-start.11) | collective-permute-done | bytes 4194336 | tf_op jit(solution)/shard_map/ppermute | solution.py:180
  548.6 4.3 copy.33
  556.0 7.1 shard_map.53
  564.8 5.6 convolution_bitcast_fusion.2
  570.3 68.1 %collective-permute-done.16.came_ref = bf16[8,64,4096]{2,1,0:T(8,128)(2,1)} collective-permute-done((bf16[8,64,4096]{2,1,0:T(8,128)(2,1)}, bf16[8,64,4096]{2,1,0:T(8,128)(2,1)}, u32[]{:S(2)}, u32[]{:S(2)}) %collective-permute-start.16) | collective-permute-done | bytes 4194336 | tf_op jit(solution)/shard_map/ppermute | solution.py:180
  638.4 3.6 shard_map.56.home_ref
  642.1 5.5 convolution_bitcast_fusion.1
  647.6 10.4 %slice_subtract_fusion = (f32[8,512,256]{2,1,0:T(8,128)}, f32[8,512,256]{2,1,0:T(8,128)}) fusion(f32[8,512,512]{2,1,0:T(8,128)} %convolution_bitcast_fusion.1, f32[8,512,512]{2,1,0:T(8,128)} %convolution_bitcast_fusion.2), kind=kLoop, calls=%fused_computation.24 | loop fusion | flops 2097152 | bytes 25165824 | tf_op jit(solution)/shard_map/sub | solution.py:266
  658.0 5.3 fusion.4.back_ref
  663.3 7.5 shard_map.58.rest_0_
  670.8 7.2 shard_map.59.rest_0_
  678.1 7.9 shard_map.60.rest_0_
  686.0 11.8 %shard_map.61.rest_0_ = bf16[8,512,4096]{2,1,0:T(8,128)(2,1)} custom-call(f32[8,1]{1,0:T(8,128)S(1)} %copy.47.bias_ref, bf16[8,512,512]{2,1,0:T(8,128)(2,1)S(1)} %copy-done, bf16[512,4096]{1,0:T(8,128)(2,1)} %maximum_multiply_fusion.2.cols_ref, bf16[8,64,4096]{2,1,0:T(8,128)(2,1)} %copy-done.1, ...), custom_call_target="tpu_custom_call", output_to_operand_aliasing={{}: (5, {})} | custom-call | flops 2147483648 | bytes 12582912 | tf_op jit(solution)/shard_map/pallas_call | solution.py:112
  697.8 5.1 shard_map.54
  706.0 11.9 %shard_map.62.rest_0_ = bf16[8,512,4096]{2,1,0:T(8,128)(2,1)} custom-call(f32[8,1]{1,0:T(8,128)S(1)} %copy.47.bias_ref, bf16[8,512,512]{2,1,0:T(8,128)(2,1)S(1)} %copy-done, bf16[512,4096]{1,0:T(8,128)(2,1)} %maximum_multiply_fusion.2.cols_ref, bf16[8,64,4096]{2,1,0:T(8,128)(2,1)} %copy-done.2, ...), custom_call_target="tpu_custom_call", output_to_operand_aliasing={{}: (5, {})} | custom-call | flops 2147483648 | bytes 12582912 | tf_op jit(solution)/shard_map/pallas_call | solution.py:112
  717.9 11.8 %shard_map.63.rest_0_ = bf16[8,512,4096]{2,1,0:T(8,128)(2,1)} custom-call(f32[8,1]{1,0:T(8,128)S(1)} %copy.47.bias_ref, bf16[8,512,512]{2,1,0:T(8,128)(2,1)S(1)} %copy-done, bf16[512,4096]{1,0:T(8,128)(2,1)} %maximum_multiply_fusion.2.cols_ref, bf16[8,64,4096]{2,1,0:T(8,128)(2,1)} %copy-done.3, ...), custom_call_target="tpu_custom_call", output_to_operand_aliasing={{}: (5, {})} | custom-call | flops 2147483648 | bytes 12582912 | tf_op jit(solution)/shard_map/pallas_call | solution.py:112
  729.7 11.8 %shard_map.64.rest_0_ = bf16[8,512,4096]{2,1,0:T(8,128)(2,1)} custom-call(f32[8,1]{1,0:T(8,128)S(1)} %copy.47.bias_ref, bf16[8,512,512]{2,1,0:T(8,128)(2,1)S(1)} %copy-done, bf16[512,4096]{1,0:T(8,128)(2,1)} %maximum_multiply_fusion.2.cols_ref, bf16[8,64,4096]{2,1,0:T(8,128)(2,1)} %copy-done.4, ...), custom_call_target="tpu_custom_call", output_to_operand_aliasing={{}: (5, {})} | custom-call | flops 2147483648 | bytes 12582912 | tf_op jit(solution)/shard_map/pallas_call | solution.py:112
  744.4 12.0 %shard_map.65.rest_0_ = bf16[8,512,4096]{2,1,0:T(8,128)(2,1)} custom-call(f32[8,1]{1,0:T(8,128)S(1)} %copy.47.bias_ref, bf16[8,512,512]{2,1,0:T(8,128)(2,1)S(1)} %copy-done, bf16[512,4096]{1,0:T(8,128)(2,1)} %maximum_multiply_fusion.2.cols_ref, bf16[8,64,4096]{2,1,0:T(8,128)(2,1)} %copy-done.5, ...), custom_call_target="tpu_custom_call", output_to_operand_aliasing={{}: (5, {})} | custom-call | flops 2147483648 | bytes 12582912 | tf_op jit(solution)/shard_map/pallas_call | solution.py:112
  756.4 11.1 %shard_map.66.rest_0_ = bf16[8,512,4096]{2,1,0:T(8,128)(2,1)} custom-call(f32[8,1]{1,0:T(8,128)S(1)} %copy.47.bias_ref, bf16[8,512,512]{2,1,0:T(8,128)(2,1)} %fusion.4.back_ref, bf16[512,4096]{1,0:T(8,128)(2,1)} %maximum_multiply_fusion.2.cols_ref, bf16[8,48,4096]{2,1,0:T(8,128)(2,1)S(1)} %copy-done.7, ...), custom_call_target="tpu_custom_call", output_to_operand_aliasing={{}: (5, {})} | custom-call | flops 1610612736 | bytes 9437184 | tf_op jit(solution)/shard_map/pallas_call | solution.py:112
  770.5 8.2 %shard_map.67.rest_0_ = bf16[8,512,4096]{2,1,0:T(8,128)(2,1)} custom-call(f32[8,1]{1,0:T(8,128)S(1)} %copy.47.bias_ref, bf16[8,512,512]{2,1,0:T(8,128)(2,1)} %fusion.4.back_ref, bf16[512,4096]{1,0:T(8,128)(2,1)} %maximum_multiply_fusion.2.cols_ref, bf16[8,32,4096]{2,1,0:T(8,128)(2,1)S(1)} %get-tuple-element.112.home_ref, ...), custom_call_target="tpu_custom_call", output_to_operand_aliasing={{}: (5, {})} | custom-call | flops 1073741824 | bytes 6291456 | tf_op jit(solution)/shard_map/pallas_call | solution.py:112
  778.7 5.7 shard_map.68
  (125 shorter events, 60.4 us)
Async XLA Ops:
  6.5 440.6 %reduce-scatter.2.cloned.1.call-start = ((), (), s32[]{:S(2)}) async-start(), calls=%async_computation.1 | async-start | bytes 4718592 | tf_op jit(solution)/shard_map/reduce_scatter | solution.py:238
  9.7 7.9 %copy-start.22 = (bf16[32,32]{1,0:T(8,128)(2,1)S(1)}, bf16[32,32]{1,0:T(8,128)(2,1)}, u32[]{:S(2)}) copy-start(bf16[32,32]{1,0:T(8,128)(2,1)} %param.6) | copy-start | bytes 6148
  14.4 6.4 collective-permute-start.2
  14.9 49.2 %collective-permute-start.4 = (bf16[8,32,4096]{2,1,0:T(8,128)(2,1)}, bf16[8,32,4096]{2,1,0:T(8,128)(2,1)S(1)}, u32[]{:S(2)}, u32[]{:S(2)}) collective-permute-start(bf16[8,32,4096]{2,1,0:T(8,128)(2,1)} %slice.69), channel_id=1, source_target_pairs={{0,2},{1,3},{2,0},{3,1},{4,6},{5,7},{6,4},{7,5},{8,10},{9,11},{10,... | collective-permute-start | bytes 6291464 | tf_op jit(solution)/shard_map/ppermute | solution.py:142
  17.4 10.1 %collective-permute-start = (bf16[8,32,4096]{2,1,0:T(8,128)(2,1)}, bf16[8,32,4096]{2,1,0:T(8,128)(2,1)}, u32[]{:S(2)}, u32[]{:S(2)}) collective-permute-start(bf16[8,32,4096]{2,1,0:T(8,128)(2,1)} %get-tuple-element.128), channel_id=1, source_target_pairs={{0,1},{1,0},{2,3},{3,2},{4,5},{5,4},{6,7},{7,6},{8,9},{9,8},{10,11... | collective-permute-start | bytes 6291464 | tf_op jit(solution)/shard_map/ppermute | solution.py:139
  26.5 82.3 %collective-permute-start.3 = (bf16[8,32,4096]{2,1,0:T(8,128)(2,1)S(1)}, bf16[8,32,4096]{2,1,0:T(8,128)(2,1)S(1)}, u32[]{:S(2)}, u32[]{:S(2)}) collective-permute-start(bf16[8,32,4096]{2,1,0:T(8,128)(2,1)S(1)} %get-tuple-element.64), channel_id=1, source_target_pairs={{0,2},{1,3},{2,0},{3,1},{4,6},{5,7},{6,4},{7,5},{8,10},{9,11},{10,... | collective-permute-start | bytes 6291464 | tf_op jit(solution)/shard_map/ppermute | solution.py:180
  32.6 83.2 %copy-start.14 = (bf16[8,32,4096]{2,1,0:T(8,128)(2,1)}, bf16[8,32,4096]{2,1,0:T(8,128)(2,1)S(1)}, u32[]{:S(2)}) copy-start(bf16[8,32,4096]{2,1,0:T(8,128)(2,1)S(1)} %get-tuple-element.104.home_ref) | copy-start | bytes 6291460
  64.1 434.0 %copy-start.8 = (bf16[8,32,4096]{2,1,0:T(8,128)(2,1)}, bf16[8,32,4096]{2,1,0:T(8,128)(2,1)S(1)}, u32[]{:S(2)}) copy-start(bf16[8,32,4096]{2,1,0:T(8,128)(2,1)S(1)} %collective-permute-done.4.one_ref) | copy-start | bytes 6291460
  108.8 6.9 copy-start.12
  115.7 7.6 collective-permute-start.5
  115.8 54.0 %collective-permute-start.6 = (bf16[8,64,4096]{2,1,0:T(8,128)(2,1)}, bf16[8,64,4096]{2,1,0:T(8,128)(2,1)}, u32[]{:S(2)}, u32[]{:S(2)}) collective-permute-start(bf16[8,64,4096]{2,1,0:T(8,128)(2,1)} %get-tuple-element.125), channel_id=1, source_target_pairs={{0,1},{1,0},{2,3},{3,2},{4,5},{5,4},{6,7},{7,6},{8,9},{9,8},{10,11... | collective-permute-start | bytes 12582920 | tf_op jit(solution)/shard_map/ppermute | solution.py:139
  116.3 48.8 %collective-permute-start.1 = (bf16[8,32,4096]{2,1,0:T(8,128)(2,1)}, bf16[8,32,4096]{2,1,0:T(8,128)(2,1)}, u32[]{:S(2)}, u32[]{:S(2)}) collective-permute-start(bf16[8,32,4096]{2,1,0:T(8,128)(2,1)} %get-tuple-element.63), channel_id=1, source_target_pairs={{0,2},{1,3},{2,0},{3,1},{4,6},{5,7},{6,4},{7,5},{8,10},{9,11},{10,... | collective-permute-start | bytes 6291464 | tf_op jit(solution)/shard_map/ppermute | solution.py:180
  130.6 39.2 %copy-start.1 = (bf16[8,64,4096]{2,1,0:T(8,128)(2,1)}, bf16[8,64,4096]{2,1,0:T(8,128)(2,1)S(1)}, u32[]{:S(2)}) copy-start(bf16[8,64,4096]{2,1,0:T(8,128)(2,1)S(1)} %get-tuple-element.102.home_ref) | copy-start | bytes 12582916
  130.6 123.5 %collective-permute-start.8 = (bf16[8,64,4096]{2,1,0:T(8,128)(2,1)S(1)}, bf16[8,64,4096]{2,1,0:T(8,128)(2,1)}, u32[]{:S(2)}, u32[]{:S(2)}) collective-permute-start(bf16[8,64,4096]{2,1,0:T(8,128)(2,1)S(1)} %get-tuple-element.72), channel_id=1, source_target_pairs={{0,2},{1,3},{2,0},{3,1},{4,6},{5,7},{6,4},{7,5},{8,10},{9,11},{10,... | collective-permute-start | bytes 12582920 | tf_op jit(solution)/shard_map/ppermute | solution.py:180
  169.8 99.7 %collective-permute-start.9 = (bf16[8,64,4096]{2,1,0:T(8,128)(2,1)}, bf16[8,64,4096]{2,1,0:T(8,128)(2,1)}, u32[]{:S(2)}, u32[]{:S(2)}) collective-permute-start(bf16[8,64,4096]{2,1,0:T(8,128)(2,1)} %slice.74), channel_id=1, source_target_pairs={{0,1},{1,0},{2,3},{3,2},{4,5},{5,4},{6,7},{7,6},{8,9},{9,8},{10,11... | collective-permute-start | bytes 12582920 | tf_op jit(solution)/shard_map/ppermute | solution.py:139
  177.1 2.0 copy-start.2
  179.1 2.0 copy-start.19
  265.1 208.0 %all-gather.3.cloned.1.call-start = ((), (), s32[]{:S(2)}) async-start(), calls=%async_computation.2 | async-start | bytes 1310720 | tf_op jit(solution)/shard_map/all_gather | solution.py:246
  265.1 93.8 %collective-permute-start.7 = (bf16[8,64,4096]{2,1,0:T(8,128)(2,1)}, bf16[8,64,4096]{2,1,0:T(8,128)(2,1)S(1)}, u32[]{:S(2)}, u32[]{:S(2)}) collective-permute-start(bf16[8,64,4096]{2,1,0:T(8,128)(2,1)} %copy-done.19), channel_id=1, source_target_pairs={{0,2},{1,3},{2,0},{3,1},{4,6},{5,7},{6,4},{7,5},{8,10},{9,11},{10,... | collective-permute-start | bytes 12582920 | tf_op jit(solution)/shard_map/ppermute | solution.py:180
  269.4 95.7 %collective-permute-start.10 = (bf16[8,64,4096]{2,1,0:T(8,128)(2,1)S(1)}, bf16[8,64,4096]{2,1,0:T(8,128)(2,1)S(1)}, u32[]{:S(2)}, u32[]{:S(2)}) collective-permute-start(bf16[8,64,4096]{2,1,0:T(8,128)(2,1)S(1)} %slice.75), channel_id=1, source_target_pairs={{0,1},{1,0},{2,3},{3,2},{4,5},{5,4},{6,7},{7,6},{8,9},{9,8},{10,11... | collective-permute-start | bytes 12582920 | tf_op jit(solution)/shard_map/ppermute | solution.py:139
  276.8 88.3 %copy-start.3 = (bf16[8,64,4096]{2,1,0:T(8,128)(2,1)}, bf16[8,64,4096]{2,1,0:T(8,128)(2,1)S(1)}, u32[]{:S(2)}) copy-start(bf16[8,64,4096]{2,1,0:T(8,128)(2,1)S(1)} %get-tuple-element.97.home_ref) | copy-start | bytes 12582916
  276.9 170.3 %collective-permute-start.12 = (bf16[8,64,4096]{2,1,0:T(8,128)(2,1)S(1)}, bf16[8,64,4096]{2,1,0:T(8,128)(2,1)}, u32[]{:S(2)}, u32[]{:S(2)}) collective-permute-start(bf16[8,64,4096]{2,1,0:T(8,128)(2,1)S(1)} %get-tuple-element.79), channel_id=1, source_target_pairs={{0,2},{1,3},{2,0},{3,1},{4,6},{5,7},{6,4},{7,5},{8,10},{9,11},{10,... | collective-permute-start | bytes 12582920 | tf_op jit(solution)/shard_map/ppermute | solution.py:180
  358.9 6.2 copy-start.21
  365.1 118.4 %collective-permute-start.13 = (bf16[8,64,4096]{2,1,0:T(8,128)(2,1)}, bf16[8,64,4096]{2,1,0:T(8,128)(2,1)}, u32[]{:S(2)}, u32[]{:S(2)}) collective-permute-start(bf16[8,64,4096]{2,1,0:T(8,128)(2,1)} %slice.80), channel_id=1, source_target_pairs={{0,1},{1,0},{2,3},{3,2},{4,5},{5,4},{6,7},{7,6},{8,9},{9,8},{10,11... | collective-permute-start | bytes 12582920 | tf_op jit(solution)/shard_map/ppermute | solution.py:139
  372.1 2.0 copy-start.4
  374.0 2.0 copy-start.18
  449.0 99.6 %all-gather.5.cloned.1.call-start = ((), (), s32[]{:S(2)}) async-start(), calls=%async_computation.3 | async-start | bytes 2359296 | tf_op jit(solution)/shard_map/all_gather | solution.py:258
  449.0 99.5 %collective-permute-start.11 = (bf16[8,64,4096]{2,1,0:T(8,128)(2,1)}, bf16[8,64,4096]{2,1,0:T(8,128)(2,1)}, u32[]{:S(2)}, u32[]{:S(2)}) collective-permute-start(bf16[8,64,4096]{2,1,0:T(8,128)(2,1)} %copy-done.18), channel_id=1, source_target_pairs={{0,2},{1,3},{2,0},{3,1},{4,6},{5,7},{6,4},{7,5},{8,10},{9,11},{10,... | collective-permute-start | bytes 12582920 | tf_op jit(solution)/shard_map/ppermute | solution.py:180
  491.9 2.0 copy-start.5
  493.9 5.2 copy-start.23
  493.9 144.5 %collective-permute-start.16 = (bf16[8,64,4096]{2,1,0:T(8,128)(2,1)}, bf16[8,64,4096]{2,1,0:T(8,128)(2,1)}, u32[]{:S(2)}, u32[]{:S(2)}) collective-permute-start(bf16[8,64,4096]{2,1,0:T(8,128)(2,1)} %get-tuple-element.88), channel_id=1, source_target_pairs={{0,2},{1,3},{2,0},{3,1},{4,6},{5,7},{6,4},{7,5},{8,10},{9,11},{10,... | collective-permute-start | bytes 12582920 | tf_op jit(solution)/shard_map/ppermute | solution.py:180
  498.1 57.9 %collective-permute-start.14 = (bf16[8,48,4096]{2,1,0:T(8,128)(2,1)}, bf16[8,48,4096]{2,1,0:T(8,128)(2,1)}, u32[]{:S(2)}, u32[]{:S(2)}) collective-permute-start(bf16[8,48,4096]{2,1,0:T(8,128)(2,1)} %slice.89), channel_id=1, source_target_pairs={{0,1},{1,0},{2,3},{3,2},{4,5},{5,4},{6,7},{7,6},{8,9},{9,8},{10,11... | collective-permute-start | bytes 9437192 | tf_op jit(solution)/shard_map/ppermute | solution.py:139
  498.1 20.6 %collective-permute-start.20 = (bf16[8,32,4096]{2,1,0:T(8,128)(2,1)S(1)}, bf16[8,32,4096]{2,1,0:T(8,128)(2,1)}, u32[]{:S(2)}, u32[]{:S(2)}) collective-permute-start(bf16[8,32,4096]{2,1,0:T(8,128)(2,1)S(1)} %collective-permute-done.4.one_ref), channel_id=1, source_target_pairs={{0,1},{1,0},{2,3},{3,2},{4,5},{5,4},{6,7},{7,6},{8,9},{9,8},{10,11... | collective-permute-start | bytes 6291464 | tf_op jit(solution)/shard_map/ppermute | solution.py:272
  499.2 139.3 %collective-permute-start.19 = (bf16[8,32,4096]{2,1,0:T(8,128)(2,1)}, bf16[8,32,4096]{2,1,0:T(8,128)(2,1)}, u32[]{:S(2)}, u32[]{:S(2)}) collective-permute-start(bf16[8,32,4096]{2,1,0:T(8,128)(2,1)} %slice.69), channel_id=1, source_target_pairs={{0,1},{1,0},{2,3},{3,2},{4,5},{5,4},{6,7},{7,6},{8,9},{9,8},{10,11... | collective-permute-start | bytes 6291464 | tf_op jit(solution)/shard_map/ppermute | solution.py:270
  516.4 2.4 copy-start.9
  556.0 8.8 %copy-start.20 = (bf16[8,256,512]{1,2,0:T(8,128)(2,1)S(1)}, bf16[8,256,512]{1,2,0:T(8,128)(2,1)}, u32[]{:S(2)}) copy-start(bf16[8,256,512]{1,2,0:T(8,128)(2,1)} %copy.33) | copy-start | bytes 6291460
  556.0 141.8 %collective-permute-start.17 = (bf16[8,32,4096]{2,1,0:T(8,128)(2,1)}, bf16[8,32,4096]{2,1,0:T(8,128)(2,1)}, u32[]{:S(2)}, u32[]{:S(2)}) collective-permute-start(bf16[8,32,4096]{2,1,0:T(8,128)(2,1)} %slice.90), channel_id=1, source_target_pairs={{0,1},{1,0},{2,3},{3,2},{4,5},{5,4},{6,7},{7,6},{8,9},{9,8},{10,11... | collective-permute-start | bytes 6291464 | tf_op jit(solution)/shard_map/ppermute | solution.py:139
  563.0 7.3 copy-start.6
  563.0 178.5 %collective-permute-start.15 = (bf16[8,48,4096]{2,1,0:T(8,128)(2,1)}, bf16[8,48,4096]{2,1,0:T(8,128)(2,1)}, u32[]{:S(2)}, u32[]{:S(2)}) collective-permute-start(bf16[8,48,4096]{2,1,0:T(8,128)(2,1)} %get-tuple-element.87), channel_id=1, source_target_pairs={{0,2},{1,3},{2,0},{3,1},{4,6},{5,7},{6,4},{7,5},{8,10},{9,11},{10,... | collective-permute-start | bytes 9437192 | tf_op jit(solution)/shard_map/ppermute | solution.py:180
  663.3 7.5 copy-start.11
  663.3 7.5 copy-start.13
  670.8 7.2 copy-start.15
  678.1 7.9 copy-start
  702.9 64.6 %collective-permute-start.22 = (bf16[8,32,4096]{2,1,0:T(8,128)(2,1)}, bf16[8,32,4096]{2,1,0:T(8,128)(2,1)S(1)}, u32[]{:S(2)}, u32[]{:S(2)}) collective-permute-start(bf16[8,32,4096]{2,1,0:T(8,128)(2,1)} %get-tuple-element.113), channel_id=1, source_target_pairs={{0,2},{1,3},{2,0},{3,1},{4,6},{5,7},{6,4},{7,5},{8,10},{9,11},{10,... | collective-permute-start | bytes 6291464 | tf_op jit(solution)/shard_map/ppermute | solution.py:180
  705.9 35.6 %collective-permute-start.18 = (bf16[8,16,4096]{2,1,0:T(8,128)(2,1)S(1)}, bf16[8,16,4096]{2,1,0:T(8,128)(2,1)S(1)}, u32[]{:S(2)}, u32[]{:S(2)}) collective-permute-start(bf16[8,16,4096]{2,1,0:T(8,128)(2,1)S(1)} %slice.91), channel_id=1, source_target_pairs={{0,1},{1,0},{2,3},{3,2},{4,5},{5,4},{6,7},{7,6},{8,9},{9,8},{10,11... | collective-permute-start | bytes 3145736 | tf_op jit(solution)/shard_map/ppermute | solution.py:139
  744.0 12.4 %copy-start.7 = (bf16[8,48,4096]{2,1,0:T(8,128)(2,1)S(1)}, bf16[8,48,4096]{2,1,0:T(8,128)(2,1)}, u32[]{:S(2)}) copy-start(bf16[8,48,4096]{2,1,0:T(8,128)(2,1)} %copy-done.6) | copy-start | bytes 9437188
  744.0 34.7 %collective-permute-start.21 = (bf16[8,16,4096]{2,1,0:T(8,128)(2,1)S(1)}, bf16[8,16,4096]{2,1,0:T(8,128)(2,1)S(1)}, u32[]{:S(2)}, u32[]{:S(2)}) collective-permute-start(bf16[8,16,4096]{2,1,0:T(8,128)(2,1)S(1)} %get-tuple-element.111), channel_id=1, source_target_pairs={{0,2},{1,3},{2,0},{3,1},{4,6},{5,7},{6,4},{7,5},{8,10},{9,11},{10,... | collective-permute-start | bytes 3145736 | tf_op jit(solution)/shard_map/ppermute | solution.py:180
  768.9 1.6 copy-start.17
  (2 other events, 2.7 us)
Sparse Core Ops, SparseCore 0:
  265.2 89.5 reduce-scatter.1
  449.1 23.9 all-gather.2
  483.7 49.2 all-gather.4

commit v3 on v2

--- a/solution.py
+++ b/solution.py
@@ -236,12 +236,9 @@
     spec_im = partial_value[:, :MX, MY:] - partial_value[:, MX:, :MY]
     partial_value = jnp.concatenate([spec_re, spec_im], -1) * (1.0 / math.sqrt(full_rows))
     block = lax.psum_scatter(partial_value, "row", scatter_dimension=1, tiled=True)
-    (image,) = gate(4, image)
+    image, block = gate(4, image, block)
     meet(7)
     issue(6)
-    image, block = gate(5, image, block)
-    meet(8)
-    issue(7)
     spectrum = block.astype(jnp.bfloat16)
     all_inputs = lax.all_gather(spectrum, "chan", axis=0, tiled=True)
     zed_re = all_inputs[..., :MY].astype(jnp.float32)
@@ -256,7 +253,10 @@
     )
     mixed = jnp.concatenate([mix_re, mix_im], -1).astype(jnp.bfloat16)
     piece = lax.all_gather(mixed, "row", axis=1, tiled=True)
-    image, piece = gate(6, image, piece)
+    image, piece = gate(5, image, piece)
+    meet(8)
+    issue(7)
+    (image,) = gate(6, image)
     meet(9)
     issue(8)
     cos_back = cos_h.T.astype(jnp.bfloat16)

time: 801 us -> 803 us (level)
    unnamed x51 -> x49, local copies, waits for them, and re-layouts: 15.4 us -> 16.5 us
  transfers between devices with their start and end apart: 26 -> 26, of which waited for: 10 -> 14; matrix products, arithmetic and copies ran while one was open for 18% -> 16% of each run, Pallas kernels for 21% -> 22%
where the time goes in v3:
time: 803 us; the launch traced here: 794 us
  waiting for transfers between devices  409 us (51%)
  Pallas kernels  177 us (22%)
  other arithmetic  71.1 us (9%)
  local copies, waits for them, and re-layouts  65.7 us (8%)
  matrix products  36.7 us (5%)
  starting transfers between devices  20.2 us (3%)
  between operations  13.9 us (2%)
    ppermute x10, waiting for transfers between devices, issue(): cames[n] = lax.ppermute(away, 'chan', chip_swap)  350 us
    pallas_call x11, Pallas kernels, finish(): pl.pallas_call(final_kernel, grid=(rows // tall,), in_specs=in_specs, out...  107 us
    pallas_call x12, Pallas kernels, partials(): pl.pallas_call(partial_kernel, grid=(rows // UNIT,), in_specs=[pl.BlockSp...  70.2 us
    another operation x3, other arithmetic  39.3 us
    slice x8, local copies, waits for them, and re-layouts, swap(): mine = lax.slice_in_dim(part, start, start + rows, axis=1)  32 us
    ppermute x1, waiting for transfers between devices, on_device(): first_far = lax.ppermute(first_mine, 'chan', chip_swap)  31.5 us
    dot_general x1, matrix products, on_device(): jnp.dot(image.reshape(chan_count * row_count, width_len), fwd_cols, prefe...  23 us
    all_gather x1, waiting for transfers between devices, on_device(): all_inputs = lax.all_gather(spectrum, 'chan', axis=0, tiled=True)  17.6 us
  transfers between devices with their start and end apart: 26, of which 14 were waited for; matrix products, arithmetic and copies ran while one was open for 16% of the time, Pallas kernels for 22%

profile of v3, /device:TPU:0, one launch (start us, length us, event | category | flops | bytes accessed | tf_op | source)
XLA Modules:
  0.0 793.7 jit_solution(1762962028509280501)
XLA Ops:
  9.7 4.8 fusion.52
  20.9 4.3 shard_map.47
  27.6 5.1 shard_map.46
  32.7 31.5 %collective-permute-done.4.one_ref = bf16[8,32,4096]{2,1,0:T(8,128)(2,1)S(1)} collective-permute-done((bf16[8,32,4096]{2,1,0:T(8,128)(2,1)}, bf16[8,32,4096]{2,1,0:T(8,128)(2,1)S(1)}, u32[]{:S(2)}, u32[]{:S(2)}) %collective-permute-start.4) | collective-permute-done | bytes 2097184 | tf_op jit(solution)/shard_map/ppermute | solution.py:142
  64.1 44.8 %collective-permute-done.3.came_ref = bf16[8,32,4096]{2,1,0:T(8,128)(2,1)S(1)} collective-permute-done((bf16[8,32,4096]{2,1,0:T(8,128)(2,1)S(1)}, bf16[8,32,4096]{2,1,0:T(8,128)(2,1)S(1)}, u32[]{:S(2)}, u32[]{:S(2)}) %collective-permute-start.3) | collective-permute-done | bytes 2097184 | tf_op jit(solution)/shard_map/ppermute | solution.py:180
  108.9 6.9 fusion.51
  118.1 5.2 collective-permute-done.5.two_ref
  123.4 7.3 shard_map.48
  132.5 19.7 %cosine_convert_fusion.1 = (bf16[4096,256]{1,0:T(8,128)(2,1)S(1)}, bf16[4096,256]{1,0:T(8,128)(2,1)}) fusion(s32[4096]{0:T(1024)S(1)} %iota.51), kind=kLoop, calls=%fused_computation.35 | loop fusion | flops 17825792 | bytes 4210688 | tf_op jit(solution)/shard_map/convert.8
  152.1 13.0 %collective-permute-done.1.came_ref = bf16[8,32,4096]{2,1,0:T(8,128)(2,1)} collective-permute-done((bf16[8,32,4096]{2,1,0:T(8,128)(2,1)}, bf16[8,32,4096]{2,1,0:T(8,128)(2,1)}, u32[]{:S(2)}, u32[]{:S(2)}) %collective-permute-start.1) | collective-permute-done | bytes 2097184 | tf_op jit(solution)/shard_map/ppermute | solution.py:180
  165.2 7.3 shard_map.49
  179.1 23.0 %multiply_convert_fusion = bf16[4096,512]{1,0:T(8,128)(2,1)S(1)} fusion(bf16[4096,4096]{1,0:T(8,128)(2,1)} %bitcast.56, bf16[4096,256]{1,0:T(8,128)(2,1)} %get-tuple-element.138, bf16[4096,256]{1,0:T(8,128)(2,1)S(1)} %get-tuple-element.137), kind=kOutput, calls=%fused_computation.10 | convolution fusion | flops 17192452096 | bytes 41943040 | tf_op jit(solution)/shard_map/dot_general | solution.py:217
  202.1 52.1 %collective-permute-done.6.came_ref = bf16[8,64,4096]{2,1,0:T(8,128)(2,1)} collective-permute-done((bf16[8,64,4096]{2,1,0:T(8,128)(2,1)S(1)}, bf16[8,64,4096]{2,1,0:T(8,128)(2,1)}, u32[]{:S(2)}, u32[]{:S(2)}) %collective-permute-start.6) | collective-permute-done | bytes 4194336 | tf_op jit(solution)/shard_map/ppermute | solution.py:180
  259.6 5.5 copy.30
  270.4 4.7 collective-permute-done.8.two_ref
  275.0 7.8 shard_map.50
  284.9 76.1 %collective-permute-done.10.came_ref = bf16[8,64,4096]{2,1,0:T(8,128)(2,1)} collective-permute-done((bf16[8,64,4096]{2,1,0:T(8,128)(2,1)S(1)}, bf16[8,64,4096]{2,1,0:T(8,128)(2,1)}, u32[]{:S(2)}, u32[]{:S(2)}) %collective-permute-start.10) | collective-permute-done | bytes 4194336 | tf_op jit(solution)/shard_map/ppermute | solution.py:180
  362.9 4.7 slice.79
  369.4 17.6 %all-gather.3.cloned.1.call-done = bf16[32,32,512]{2,1,0:T(8,128)(2,1)} async-done(((bf16[8,32,512]{2,1,0:T(8,128)(2,1)}), bf16[32,32,512]{2,1,0:T(8,128)(2,1)}) %all-gather.3.cloned.1.call-update) | async-done | bytes 1048592 | tf_op jit(solution)/shard_map/all_gather | solution.py:243
  389.7 6.6 fusion
  397.5 4.7 slice.88
  402.4 8.4 %shard_map.51 = (bf16[8,64,4096]{2,1,0:T(8,128)(2,1)}, bf16[8,64,4096]{2,1,0:T(8,128)(2,1)S(1)}) custom-call(bf16[8,512,4096]{2,1,0:T(8,128)(2,1)} %one_ref.10, bf16[8,64,4096]{2,1,0:T(8,128)(2,1)} %collective-permute-done.11.two_ref, bf16[256,256]{1,0:T(8,128)(2,1)S(1)} %constant_dynamic-update-slice_fusion.kron_ref), custom_call_target="tpu_custom_call" | custom-call | flops 2147483648 | bytes 16777216 | tf_op jit(solution)/shard_map/pallas_call | solution.py:55
  413.3 53.6 %collective-permute-done.9.came_ref = bf16[8,64,4096]{2,1,0:T(8,128)(2,1)} collective-permute-done((bf16[8,64,4096]{2,1,0:T(8,128)(2,1)}, bf16[8,64,4096]{2,1,0:T(8,128)(2,1)}, u32[]{:S(2)}, u32[]{:S(2)}) %collective-permute-start.9) | collective-permute-done | bytes 4194336 | tf_op jit(solution)/shard_map/ppermute | solution.py:180
  471.3 8.4 %shard_map.52 = (bf16[8,64,4096]{2,1,0:T(8,128)(2,1)}, bf16[8,64,4096]{2,1,0:T(8,128)(2,1)S(1)}) custom-call(bf16[8,512,4096]{2,1,0:T(8,128)(2,1)} %one_ref.10, bf16[8,64,4096]{2,1,0:T(8,128)(2,1)} %collective-permute-done.13.two_ref, bf16[256,256]{1,0:T(8,128)(2,1)S(1)} %constant_dynamic-update-slice_fusion.kron_ref), custom_call_target="tpu_custom_call" | custom-call | flops 2147483648 | bytes 16777216 | tf_op jit(solution)/shard_map/pallas_call | solution.py:55
  484.0 17.2 %cosine_convert_fusion = (bf16[256,4096]{1,0:T(8,128)(2,1)S(1)}, bf16[256,4096]{1,0:T(8,128)(2,1)S(1)}) fusion(s32[4096]{0:T(1024)S(1)} %iota.51), kind=kLoop, calls=%fused_computation.31 | loop fusion | flops 17825792 | bytes 4210688 | tf_op jit(solution)/shard_map/convert
  507.1 49.7 %collective-permute-done.12.came_ref = bf16[8,64,4096]{2,1,0:T(8,128)(2,1)} collective-permute-done((bf16[8,64,4096]{2,1,0:T(8,128)(2,1)}, bf16[8,64,4096]{2,1,0:T(8,128)(2,1)}, u32[]{:S(2)}, u32[]{:S(2)}) %collective-permute-start.12) | collective-permute-done | bytes 4194336 | tf_op jit(solution)/shard_map/ppermute | solution.py:180
  556.8 4.3 copy.33
  564.2 7.2 shard_map.53
  573.2 5.6 convolution_bitcast_fusion.2
  582.4 5.8 convolution_bitcast_fusion.1
  588.1 10.3 %slice_subtract_fusion = (f32[8,512,256]{2,1,0:T(8,128)}, f32[8,512,256]{2,1,0:T(8,128)}) fusion(f32[8,512,512]{2,1,0:T(8,128)} %convolution_bitcast_fusion.1, f32[8,512,512]{2,1,0:T(8,128)} %convolution_bitcast_fusion.2), kind=kLoop, calls=%fused_computation.24 | loop fusion | flops 2097152 | bytes 25165824 | tf_op jit(solution)/shard_map/sub | solution.py:266
  598.5 5.3 fusion.4.back_ref
  603.8 7.2 shard_map.58.rest_0_
  611.1 7.2 shard_map.59.rest_0_
  618.3 7.9 shard_map.60.rest_0_
  626.2 11.8 %shard_map.61.rest_0_ = bf16[8,512,4096]{2,1,0:T(8,128)(2,1)} custom-call(f32[8,1]{1,0:T(8,128)S(1)} %copy.47.bias_ref, bf16[8,512,512]{2,1,0:T(8,128)(2,1)S(1)} %copy-done, bf16[512,4096]{1,0:T(8,128)(2,1)} %maximum_multiply_fusion.2.cols_ref, bf16[8,64,4096]{2,1,0:T(8,128)(2,1)} %copy-done.2, ...), custom_call_target="tpu_custom_call", output_to_operand_aliasing={{}: (5, {})} | custom-call | flops 2147483648 | bytes 12582912 | tf_op jit(solution)/shard_map/pallas_call | solution.py:112
  638.0 8.7 %collective-permute-done.16.came_ref = bf16[8,64,4096]{2,1,0:T(8,128)(2,1)} collective-permute-done((bf16[8,64,4096]{2,1,0:T(8,128)(2,1)}, bf16[8,64,4096]{2,1,0:T(8,128)(2,1)}, u32[]{:S(2)}, u32[]{:S(2)}) %collective-permute-start.16) | collective-permute-done | bytes 4194336 | tf_op jit(solution)/shard_map/ppermute | solution.py:180
  646.7 5.1 shard_map.54
  654.9 11.9 %shard_map.62.rest_0_ = bf16[8,512,4096]{2,1,0:T(8,128)(2,1)} custom-call(f32[8,1]{1,0:T(8,128)S(1)} %copy.47.bias_ref, bf16[8,512,512]{2,1,0:T(8,128)(2,1)S(1)} %copy-done, bf16[512,4096]{1,0:T(8,128)(2,1)} %maximum_multiply_fusion.2.cols_ref, bf16[8,64,4096]{2,1,0:T(8,128)(2,1)} %copy-done.1, ...), custom_call_target="tpu_custom_call", output_to_operand_aliasing={{}: (5, {})} | custom-call | flops 2147483648 | bytes 12582912 | tf_op jit(solution)/shard_map/pallas_call | solution.py:112
  666.8 11.8 %shard_map.63.rest_0_ = bf16[8,512,4096]{2,1,0:T(8,128)(2,1)} custom-call(f32[8,1]{1,0:T(8,128)S(1)} %copy.47.bias_ref, bf16[8,512,512]{2,1,0:T(8,128)(2,1)S(1)} %copy-done, bf16[512,4096]{1,0:T(8,128)(2,1)} %maximum_multiply_fusion.2.cols_ref, bf16[8,64,4096]{2,1,0:T(8,128)(2,1)} %copy-done.3, ...), custom_call_target="tpu_custom_call", output_to_operand_aliasing={{}: (5, {})} | custom-call | flops 2147483648 | bytes 12582912 | tf_op jit(solution)/shard_map/pallas_call | solution.py:112
  678.6 11.8 %shard_map.64.rest_0_ = bf16[8,512,4096]{2,1,0:T(8,128)(2,1)} custom-call(f32[8,1]{1,0:T(8,128)S(1)} %copy.47.bias_ref, bf16[8,512,512]{2,1,0:T(8,128)(2,1)S(1)} %copy-done, bf16[512,4096]{1,0:T(8,128)(2,1)} %maximum_multiply_fusion.2.cols_ref, bf16[8,64,4096]{2,1,0:T(8,128)(2,1)} %copy-done.4, ...), custom_call_target="tpu_custom_call", output_to_operand_aliasing={{}: (5, {})} | custom-call | flops 2147483648 | bytes 12582912 | tf_op jit(solution)/shard_map/pallas_call | solution.py:112
  690.4 23.7 %collective-permute-done.15.came_ref = bf16[8,48,4096]{2,1,0:T(8,128)(2,1)} collective-permute-done((bf16[8,48,4096]{2,1,0:T(8,128)(2,1)}, bf16[8,48,4096]{2,1,0:T(8,128)(2,1)}, u32[]{:S(2)}, u32[]{:S(2)}) %collective-permute-start.15) | collective-permute-done | bytes 3145760 | tf_op jit(solution)/shard_map/ppermute | solution.py:180
  718.4 11.8 %shard_map.65.rest_0_ = bf16[8,512,4096]{2,1,0:T(8,128)(2,1)} custom-call(f32[8,1]{1,0:T(8,128)S(1)} %copy.47.bias_ref, bf16[8,512,512]{2,1,0:T(8,128)(2,1)S(1)} %copy-done, bf16[512,4096]{1,0:T(8,128)(2,1)} %maximum_multiply_fusion.2.cols_ref, bf16[8,64,4096]{2,1,0:T(8,128)(2,1)} %copy-done.5, ...), custom_call_target="tpu_custom_call", output_to_operand_aliasing={{}: (5, {})} | custom-call | flops 2147483648 | bytes 12582912 | tf_op jit(solution)/shard_map/pallas_call | solution.py:112
  730.2 11.1 %shard_map.66.rest_0_ = bf16[8,512,4096]{2,1,0:T(8,128)(2,1)} custom-call(f32[8,1]{1,0:T(8,128)S(1)} %copy.47.bias_ref, bf16[8,512,512]{2,1,0:T(8,128)(2,1)} %fusion.4.back_ref, bf16[512,4096]{1,0:T(8,128)(2,1)} %maximum_multiply_fusion.2.cols_ref, bf16[8,48,4096]{2,1,0:T(8,128)(2,1)S(1)} %copy-done.7, ...), custom_call_target="tpu_custom_call", output_to_operand_aliasing={{}: (5, {})} | custom-call | flops 1610612736 | bytes 9437184 | tf_op jit(solution)/shard_map/pallas_call | solution.py:112
  741.3 17.6 %collective-permute-done.22.came_ref = bf16[8,32,4096]{2,1,0:T(8,128)(2,1)S(1)} collective-permute-done((bf16[8,32,4096]{2,1,0:T(8,128)(2,1)}, bf16[8,32,4096]{2,1,0:T(8,128)(2,1)S(1)}, u32[]{:S(2)}, u32[]{:S(2)}) %collective-permute-start.22) | collective-permute-done | bytes 2097184 | tf_op jit(solution)/shard_map/ppermute | solution.py:180
  761.9 8.2 %shard_map.67.rest_0_ = bf16[8,512,4096]{2,1,0:T(8,128)(2,1)} custom-call(f32[8,1]{1,0:T(8,128)S(1)} %copy.47.bias_ref, bf16[8,512,512]{2,1,0:T(8,128)(2,1)} %fusion.4.back_ref, bf16[512,4096]{1,0:T(8,128)(2,1)} %maximum_multiply_fusion.2.cols_ref, bf16[8,32,4096]{2,1,0:T(8,128)(2,1)S(1)} %get-tuple-element.112.home_ref, ...), custom_call_target="tpu_custom_call", output_to_operand_aliasing={{}: (5, {})} | custom-call | flops 1073741824 | bytes 6291456 | tf_op jit(solution)/shard_map/pallas_call | solution.py:112
  770.1 10.9 %collective-permute-done.21.came_ref = bf16[8,16,4096]{2,1,0:T(8,128)(2,1)S(1)} collective-permute-done((bf16[8,16,4096]{2,1,0:T(8,128)(2,1)S(1)}, bf16[8,16,4096]{2,1,0:T(8,128)(2,1)S(1)}, u32[]{:S(2)}, u32[]{:S(2)}) %collective-permute-start.21) | collective-permute-done | bytes 1048608 | tf_op jit(solution)/shard_map/ppermute | solution.py:180
  781.0 5.7 shard_map.68
  (123 shorter events, 79.0 us)
Async XLA Ops:
  6.5 354.5 %reduce-scatter.2.cloned.1.call-start = ((), (), s32[]{:S(2)}) async-start(), calls=%async_computation.1 | async-start | bytes 4718592 | tf_op jit(solution)/shard_map/reduce_scatter | solution.py:238
  9.7 8.0 %copy-start.21 = (bf16[32,32]{1,0:T(8,128)(2,1)S(1)}, bf16[32,32]{1,0:T(8,128)(2,1)}, u32[]{:S(2)}) copy-start(bf16[32,32]{1,0:T(8,128)(2,1)} %param.6) | copy-start | bytes 6148
  14.5 6.4 collective-permute-start.2
  14.9 49.2 %collective-permute-start.4 = (bf16[8,32,4096]{2,1,0:T(8,128)(2,1)}, bf16[8,32,4096]{2,1,0:T(8,128)(2,1)S(1)}, u32[]{:S(2)}, u32[]{:S(2)}) collective-permute-start(bf16[8,32,4096]{2,1,0:T(8,128)(2,1)} %slice.69), channel_id=1, source_target_pairs={{0,2},{1,3},{2,0},{3,1},{4,6},{5,7},{6,4},{7,5},{8,10},{9,11},{10,... | collective-permute-start | bytes 6291464 | tf_op jit(solution)/shard_map/ppermute | solution.py:142
  17.5 10.2 %collective-permute-start = (bf16[8,32,4096]{2,1,0:T(8,128)(2,1)}, bf16[8,32,4096]{2,1,0:T(8,128)(2,1)}, u32[]{:S(2)}, u32[]{:S(2)}) collective-permute-start(bf16[8,32,4096]{2,1,0:T(8,128)(2,1)} %get-tuple-element.127), channel_id=1, source_target_pairs={{0,1},{1,0},{2,3},{3,2},{4,5},{5,4},{6,7},{7,6},{8,9},{9,8},{10,11... | collective-permute-start | bytes 6291464 | tf_op jit(solution)/shard_map/ppermute | solution.py:139
  26.6 82.3 %collective-permute-start.3 = (bf16[8,32,4096]{2,1,0:T(8,128)(2,1)S(1)}, bf16[8,32,4096]{2,1,0:T(8,128)(2,1)S(1)}, u32[]{:S(2)}, u32[]{:S(2)}) collective-permute-start(bf16[8,32,4096]{2,1,0:T(8,128)(2,1)S(1)} %get-tuple-element.64), channel_id=1, source_target_pairs={{0,2},{1,3},{2,0},{3,1},{4,6},{5,7},{6,4},{7,5},{8,10},{9,11},{10,... | collective-permute-start | bytes 6291464 | tf_op jit(solution)/shard_map/ppermute | solution.py:180
  32.7 83.1 %copy-start.14 = (bf16[8,32,4096]{2,1,0:T(8,128)(2,1)}, bf16[8,32,4096]{2,1,0:T(8,128)(2,1)S(1)}, u32[]{:S(2)}) copy-start(bf16[8,32,4096]{2,1,0:T(8,128)(2,1)S(1)} %get-tuple-element.104.home_ref) | copy-start | bytes 6291460
  64.1 406.6 %copy-start.8 = (bf16[8,32,4096]{2,1,0:T(8,128)(2,1)}, bf16[8,32,4096]{2,1,0:T(8,128)(2,1)S(1)}, u32[]{:S(2)}) copy-start(bf16[8,32,4096]{2,1,0:T(8,128)(2,1)S(1)} %collective-permute-done.4.one_ref) | copy-start | bytes 6291460
  108.9 6.9 copy-start.12
  115.8 7.6 collective-permute-start.5
  115.9 49.3 %collective-permute-start.7 = (bf16[8,64,4096]{2,1,0:T(8,128)(2,1)}, bf16[8,64,4096]{2,1,0:T(8,128)(2,1)}, u32[]{:S(2)}, u32[]{:S(2)}) collective-permute-start(bf16[8,64,4096]{2,1,0:T(8,128)(2,1)} %get-tuple-element.125), channel_id=1, source_target_pairs={{0,1},{1,0},{2,3},{3,2},{4,5},{5,4},{6,7},{7,6},{8,9},{9,8},{10,11... | collective-permute-start | bytes 12582920 | tf_op jit(solution)/shard_map/ppermute | solution.py:139
  116.4 48.8 %collective-permute-start.1 = (bf16[8,32,4096]{2,1,0:T(8,128)(2,1)}, bf16[8,32,4096]{2,1,0:T(8,128)(2,1)}, u32[]{:S(2)}, u32[]{:S(2)}) collective-permute-start(bf16[8,32,4096]{2,1,0:T(8,128)(2,1)} %get-tuple-element.63), channel_id=1, source_target_pairs={{0,2},{1,3},{2,0},{3,1},{4,6},{5,7},{6,4},{7,5},{8,10},{9,11},{10,... | collective-permute-start | bytes 6291464 | tf_op jit(solution)/shard_map/ppermute | solution.py:180
  130.7 34.5 %copy-start.2 = (bf16[8,64,4096]{2,1,0:T(8,128)(2,1)}, bf16[8,64,4096]{2,1,0:T(8,128)(2,1)S(1)}, u32[]{:S(2)}) copy-start(bf16[8,64,4096]{2,1,0:T(8,128)(2,1)S(1)} %get-tuple-element.102.home_ref) | copy-start | bytes 12582916
  130.7 123.5 %collective-permute-start.6 = (bf16[8,64,4096]{2,1,0:T(8,128)(2,1)S(1)}, bf16[8,64,4096]{2,1,0:T(8,128)(2,1)}, u32[]{:S(2)}, u32[]{:S(2)}) collective-permute-start(bf16[8,64,4096]{2,1,0:T(8,128)(2,1)S(1)} %get-tuple-element.70), channel_id=1, source_target_pairs={{0,2},{1,3},{2,0},{3,1},{4,6},{5,7},{6,4},{7,5},{8,10},{9,11},{10,... | collective-permute-start | bytes 12582920 | tf_op jit(solution)/shard_map/ppermute | solution.py:180
  172.5 2.1 copy-start.1
  174.5 2.0 copy-start.18
  265.1 121.8 %all-gather.3.cloned.1.call-start = ((), (), s32[]{:S(2)}) async-start(), calls=%async_computation.2 | async-start | bytes 1310720 | tf_op jit(solution)/shard_map/all_gather | solution.py:243
  265.2 3.5 copy-start.19
  267.8 7.2 collective-permute-start.8
  268.6 92.3 %collective-permute-start.10 = (bf16[8,64,4096]{2,1,0:T(8,128)(2,1)S(1)}, bf16[8,64,4096]{2,1,0:T(8,128)(2,1)}, u32[]{:S(2)}, u32[]{:S(2)}) collective-permute-start(bf16[8,64,4096]{2,1,0:T(8,128)(2,1)S(1)} %copy-done.19), channel_id=1, source_target_pairs={{0,2},{1,3},{2,0},{3,1},{4,6},{5,7},{6,4},{7,5},{8,10},{9,11},{10,... | collective-permute-start | bytes 12582920 | tf_op jit(solution)/shard_map/ppermute | solution.py:180
  282.8 2.1 copy-start.3
  362.9 104.1 %all-gather.5.cloned.1.call-start = ((), (), s32[]{:S(2)}) async-start(), calls=%async_computation.3 | async-start | bytes 2359296 | tf_op jit(solution)/shard_map/all_gather | solution.py:255
  367.6 34.8 %collective-permute-start.11 = (bf16[8,64,4096]{2,1,0:T(8,128)(2,1)}, bf16[8,64,4096]{2,1,0:T(8,128)(2,1)}, u32[]{:S(2)}, u32[]{:S(2)}) collective-permute-start(bf16[8,64,4096]{2,1,0:T(8,128)(2,1)} %slice.79), channel_id=1, source_target_pairs={{0,1},{1,0},{2,3},{3,2},{4,5},{5,4},{6,7},{7,6},{8,9},{9,8},{10,11... | collective-permute-start | bytes 12582920 | tf_op jit(solution)/shard_map/ppermute | solution.py:139
  367.6 99.3 %collective-permute-start.9 = (bf16[8,64,4096]{2,1,0:T(8,128)(2,1)}, bf16[8,64,4096]{2,1,0:T(8,128)(2,1)}, u32[]{:S(2)}, u32[]{:S(2)}) collective-permute-start(bf16[8,64,4096]{2,1,0:T(8,128)(2,1)} %get-tuple-element.75), channel_id=1, source_target_pairs={{0,2},{1,3},{2,0},{3,1},{4,6},{5,7},{6,4},{7,5},{8,10},{9,11},{10,... | collective-permute-start | bytes 12582920 | tf_op jit(solution)/shard_map/ppermute | solution.py:180
  402.2 69.1 %collective-permute-start.13 = (bf16[8,64,4096]{2,1,0:T(8,128)(2,1)}, bf16[8,64,4096]{2,1,0:T(8,128)(2,1)}, u32[]{:S(2)}, u32[]{:S(2)}) collective-permute-start(bf16[8,64,4096]{2,1,0:T(8,128)(2,1)} %slice.88), channel_id=1, source_target_pairs={{0,1},{1,0},{2,3},{3,2},{4,5},{5,4},{6,7},{7,6},{8,9},{9,8},{10,11... | collective-permute-start | bytes 12582920 | tf_op jit(solution)/shard_map/ppermute | solution.py:139
  410.8 2.1 copy-start.4
  412.9 143.9 %collective-permute-start.12 = (bf16[8,64,4096]{2,1,0:T(8,128)(2,1)}, bf16[8,64,4096]{2,1,0:T(8,128)(2,1)}, u32[]{:S(2)}, u32[]{:S(2)}) collective-permute-start(bf16[8,64,4096]{2,1,0:T(8,128)(2,1)} %get-tuple-element.83), channel_id=1, source_target_pairs={{0,2},{1,3},{2,0},{3,1},{4,6},{5,7},{6,4},{7,5},{8,10},{9,11},{10,... | collective-permute-start | bytes 12582920 | tf_op jit(solution)/shard_map/ppermute | solution.py:180
  470.8 13.1 %copy-start.22 = (f32[8]{0:T(128)S(1)}, f32[8]{0:T(128)}, u32[]{:S(2)}) copy-start(f32[8]{0:T(128)} %param.7) | copy-start | bytes 100
  470.8 93.5 %collective-permute-start.14 = (bf16[8,48,4096]{2,1,0:T(8,128)(2,1)}, bf16[8,48,4096]{2,1,0:T(8,128)(2,1)}, u32[]{:S(2)}, u32[]{:S(2)}) collective-permute-start(bf16[8,48,4096]{2,1,0:T(8,128)(2,1)} %slice.89), channel_id=1, source_target_pairs={{0,1},{1,0},{2,3},{3,2},{4,5},{5,4},{6,7},{7,6},{8,9},{9,8},{10,11... | collective-permute-start | bytes 9437192 | tf_op jit(solution)/shard_map/ppermute | solution.py:139
  470.8 32.9 %collective-permute-start.20 = (bf16[8,32,4096]{2,1,0:T(8,128)(2,1)S(1)}, bf16[8,32,4096]{2,1,0:T(8,128)(2,1)}, u32[]{:S(2)}, u32[]{:S(2)}) collective-permute-start(bf16[8,32,4096]{2,1,0:T(8,128)(2,1)S(1)} %collective-permute-done.4.one_ref), channel_id=1, source_target_pairs={{0,1},{1,0},{2,3},{3,2},{4,5},{5,4},{6,7},{7,6},{8,9},{9,8},{10,11... | collective-permute-start | bytes 6291464 | tf_op jit(solution)/shard_map/ppermute | solution.py:272
  479.7 2.0 copy-start.5
  481.6 165.1 %collective-permute-start.16 = (bf16[8,64,4096]{2,1,0:T(8,128)(2,1)}, bf16[8,64,4096]{2,1,0:T(8,128)(2,1)}, u32[]{:S(2)}, u32[]{:S(2)}) collective-permute-start(bf16[8,64,4096]{2,1,0:T(8,128)(2,1)} %get-tuple-element.88), channel_id=1, source_target_pairs={{0,2},{1,3},{2,0},{3,1},{4,6},{5,7},{6,4},{7,5},{8,10},{9,11},{10,... | collective-permute-start | bytes 12582920 | tf_op jit(solution)/shard_map/ppermute | solution.py:180
  483.9 94.8 %collective-permute-start.19 = (bf16[8,32,4096]{2,1,0:T(8,128)(2,1)}, bf16[8,32,4096]{2,1,0:T(8,128)(2,1)}, u32[]{:S(2)}, u32[]{:S(2)}) collective-permute-start(bf16[8,32,4096]{2,1,0:T(8,128)(2,1)} %slice.69), channel_id=1, source_target_pairs={{0,1},{1,0},{2,3},{3,2},{4,5},{5,4},{6,7},{7,6},{8,9},{9,8},{10,11... | collective-permute-start | bytes 6291464 | tf_op jit(solution)/shard_map/ppermute | solution.py:270
  501.1 2.6 copy-start.9
  564.2 8.9 %copy-start.20 = (bf16[8,256,512]{1,2,0:T(8,128)(2,1)S(1)}, bf16[8,256,512]{1,2,0:T(8,128)(2,1)}, u32[]{:S(2)}) copy-start(bf16[8,256,512]{1,2,0:T(8,128)(2,1)} %copy.33) | copy-start | bytes 6291460
  564.2 82.5 %collective-permute-start.17 = (bf16[8,32,4096]{2,1,0:T(8,128)(2,1)}, bf16[8,32,4096]{2,1,0:T(8,128)(2,1)}, u32[]{:S(2)}, u32[]{:S(2)}) collective-permute-start(bf16[8,32,4096]{2,1,0:T(8,128)(2,1)} %slice.90), channel_id=1, source_target_pairs={{0,1},{1,0},{2,3},{3,2},{4,5},{5,4},{6,7},{7,6},{8,9},{9,8},{10,11... | collective-permute-start | bytes 6291464 | tf_op jit(solution)/shard_map/ppermute | solution.py:139
  571.4 7.3 copy-start.6
  571.4 142.7 %collective-permute-start.15 = (bf16[8,48,4096]{2,1,0:T(8,128)(2,1)}, bf16[8,48,4096]{2,1,0:T(8,128)(2,1)}, u32[]{:S(2)}, u32[]{:S(2)}) collective-permute-start(bf16[8,48,4096]{2,1,0:T(8,128)(2,1)} %get-tuple-element.87), channel_id=1, source_target_pairs={{0,2},{1,3},{2,0},{3,1},{4,6},{5,7},{6,4},{7,5},{8,10},{9,11},{10,... | collective-permute-start | bytes 9437192 | tf_op jit(solution)/shard_map/ppermute | solution.py:180
  603.8 7.2 copy-start.11
  603.8 7.2 copy-start.13
  611.0 7.2 copy-start.15
  618.3 7.9 copy-start
  651.8 107.2 %collective-permute-start.22 = (bf16[8,32,4096]{2,1,0:T(8,128)(2,1)}, bf16[8,32,4096]{2,1,0:T(8,128)(2,1)S(1)}, u32[]{:S(2)}, u32[]{:S(2)}) collective-permute-start(bf16[8,32,4096]{2,1,0:T(8,128)(2,1)} %get-tuple-element.113), channel_id=1, source_target_pairs={{0,2},{1,3},{2,0},{3,1},{4,6},{5,7},{6,4},{7,5},{8,10},{9,11},{10,... | collective-permute-start | bytes 6291464 | tf_op jit(solution)/shard_map/ppermute | solution.py:180
  654.8 59.3 %collective-permute-start.18 = (bf16[8,16,4096]{2,1,0:T(8,128)(2,1)S(1)}, bf16[8,16,4096]{2,1,0:T(8,128)(2,1)S(1)}, u32[]{:S(2)}, u32[]{:S(2)}) collective-permute-start(bf16[8,16,4096]{2,1,0:T(8,128)(2,1)S(1)} %slice.91), channel_id=1, source_target_pairs={{0,1},{1,0},{2,3},{3,2},{4,5},{5,4},{6,7},{7,6},{8,9},{9,8},{10,11... | collective-permute-start | bytes 3145736 | tf_op jit(solution)/shard_map/ppermute | solution.py:139
  716.6 13.7 %copy-start.7 = (bf16[8,48,4096]{2,1,0:T(8,128)(2,1)S(1)}, bf16[8,48,4096]{2,1,0:T(8,128)(2,1)}, u32[]{:S(2)}) copy-start(bf16[8,48,4096]{2,1,0:T(8,128)(2,1)} %copy-done.6) | copy-start | bytes 9437188
  716.6 64.5 %collective-permute-start.21 = (bf16[8,16,4096]{2,1,0:T(8,128)(2,1)S(1)}, bf16[8,16,4096]{2,1,0:T(8,128)(2,1)S(1)}, u32[]{:S(2)}, u32[]{:S(2)}) collective-permute-start(bf16[8,16,4096]{2,1,0:T(8,128)(2,1)S(1)} %get-tuple-element.111), channel_id=1, source_target_pairs={{0,2},{1,3},{2,0},{3,1},{4,6},{5,7},{6,4},{7,5},{8,10},{9,11},{10,... | collective-permute-start | bytes 3145736 | tf_op jit(solution)/shard_map/ppermute | solution.py:180
  758.9 1.4 copy-start.16
  760.3 1.6 copy-start.17
  (1 other events, 1.3 us)
Sparse Core Ops, SparseCore 0:
  265.3 89.3 reduce-scatter.1
  363.0 23.9 all-gather.2
  397.6 49.2 all-gather.4
